TPU v7x, 256 devices: a whole 4x4x8 slice. The times are simulated.
256 devices in a mesh: replica: 4 (over x_lo, core), fsdp: 64 (over z, y, x_hi).
Axes of the slice: x: 4 (x_hi: 2, x_lo: 2; x = x_hi * 2 + x_lo), y: 4, z: 8, core: 2. Of those that a mesh axis runs over, the one named last changes fastest.
Arguments:
- global_frag: float32 [2048, 8192], P('fsdp'), may hold values from -6 to 6
- local_frag: float32 [4, 2048, 8192], P('replica', 'fsdp'), may hold values from -6 to 6
- outer_mom: float32 [2048, 8192], P('fsdp'), may hold values from -6 to 6
- grads: bfloat16 [4, 64, 256, 8192], P('replica', 'fsdp'), may hold values from -512 to 512
- inner_param: float32 [4, 256, 8192], P('replica', 'fsdp'), may hold values from -6 to 6
- inner_m: float32 [4, 256, 8192], P('replica', 'fsdp'), may hold values from -6 to 6
- inner_v: float32 [4, 256, 8192], P('replica', 'fsdp'), may hold values from 0.05 to 4
Outputs:
- new_global: float32 [2048, 8192], P('fsdp')
- new_mom: float32 [2048, 8192], P('fsdp')
- new_param: float32 [4, 256, 8192], P('replica', 'fsdp')
- new_m: float32 [4, 256, 8192], P('replica', 'fsdp')
- new_v: float32 [4, 256, 8192], P('replica', 'fsdp')
All inputs are finite; a program needn't handle non-finite values.
Results may differ from a plain program's by a relative error of at most 0.0065.
Values may be sent and summed in bfloat16 or wider, within the bound.
No kernel may reach another device: no remote copies, remote signals or barrier semaphores. Data moves between devices by JAX's collectives and lax.ppermute only.
A program may use at most 128 MiB of HBM per device.

v0:
```python
import jax
import jax.numpy as jnp
from jax import lax
from jax.sharding import PartitionSpec as P

BLOCK = 128
STEP = 8


def on_device(global_frag, local_frag, outer_mom, grads, inner_param, inner_m, inner_v):
    frag_rows = global_frag.shape[0]
    width = global_frag.shape[1]
    groups = lax.axis_size("fsdp")
    local_grad = grads[0, 0]
    delta = global_frag - local_frag[0]
    blocks = delta.reshape(frag_rows, width // BLOCK, BLOCK)
    amax = jnp.max(jnp.abs(blocks), axis=-1)
    scale = ((amax + 1e-06) / 448.0).astype(jnp.bfloat16)
    encoded = (blocks / scale.astype(jnp.float32)[..., None]).astype(jnp.bfloat16)
    decoded = encoded.astype(jnp.float32) * scale.astype(jnp.float32)[..., None]
    total = lax.psum(decoded, "replica")
    average = (0.25 * total).reshape(frag_rows, width)
    new_mom = 0.9 * outer_mom + average
    new_global = global_frag - 0.7 * (average + 0.9 * new_mom)
    summed = lax.psum_scatter(
        local_grad.astype(jnp.float32), "fsdp", scatter_dimension=0, tiled=True
    )
    gmean = (summed / groups)[None]
    new_m = 0.9 * inner_m + 0.1 * gmean
    new_v = 0.95 * inner_v + 0.05 * gmean * gmean
    m_hat = new_m / (1.0 - 0.9**STEP)
    v_hat = new_v / (1.0 - 0.95**STEP)
    new_param = inner_param - 0.0003 * (m_hat / (jnp.sqrt(v_hat) + 1e-08) + 0.1 * inner_param)
    return (new_global, new_mom, new_param, new_m, new_v)


def solution(mesh):
    placed = (
        P("fsdp", None),
        P("replica", "fsdp", None),
        P("fsdp", None),
        P("replica", "fsdp", None, None),
        P("replica", "fsdp", None),
        P("replica", "fsdp", None),
        P("replica", "fsdp", None),
    )
    return jax.shard_map(
        on_device,
        mesh=mesh,
        in_specs=placed,
        out_specs=(
            P("fsdp", None),
            P("fsdp", None),
            P("replica", "fsdp", None),
            P("replica", "fsdp", None),
            P("replica", "fsdp", None),
        ),
        check_vma=False,
    )
```

profile of v0, /device:TPU:24, one launch (start us, length us, event | category | flops | bytes accessed | tf_op | source)
XLA Modules:
  0.0 796.4 jit_solution(7098713225471709608)
XLA Ops:
  7.2 0.0 all-reduce.4.cloned.1.call-start
  7.2 1.6 fusion.2
  8.9 0.2 copy.12
  9.1 0.3 abs_reduce_fusion
  9.4 1.3 convert_multiply_fusion
  10.7 0.0 all-reduce.4.cloned.1.call-update
  10.8 0.0 copy-start.5
  10.8 0.0 all-reduce.6.cloned.1.call-start
  10.8 6.4 bitcast_convert_fusion
  17.2 0.0 copy-start
  17.2 0.0 copy-start.1
  17.2 0.0 copy-start.2
  17.2 0.0 copy-start.3
  17.2 0.0 copy-start.4
  17.2 0.0 all-reduce.6.cloned.1.call-update
  17.3 0.0 copy-done.5
  17.3 0.6 dynamic-slice
  18.6 41.9 %all-reduce.4.cloned.1.call-done = f32[32,64,128]{2,1,0:T(8,128)} async-done(((f32[32,64,128]{2,1,0:T(8,128)}), f32[32,64,128]{2,1,0:T(8,128)}) %all-reduce.4.cloned.1.call-update) | async-done | bytes 1048592 | tf_op jit(solution)/shard_map/psum | solution.py:21
  60.6 1.3 broadcast_multiply_fusion
  61.9 0.0 copy-done
  61.9 0.0 copy-done.1
  61.9 2.2 fusion.1
  64.1 723.6 %all-reduce.6.cloned.1.call-done = f32[256,8192]{1,0:T(8,128)} async-done(((f32[256,8192]{1,0:T(8,128)}), f32[256,8192]{1,0:T(8,128)}) %all-reduce.6.cloned.1.call-update) | async-done | bytes 8388624
  787.7 0.0 copy-done.2
  787.7 0.0 copy-done.3
  787.7 0.0 copy-done.4
  787.7 1.9 multiply_subtract_fusion
  (1 shorter events, 0.0 us)
Async XLA Ops:
  7.2 53.4 %all-reduce.4.cloned.1.call-start = ((), (), s32[]{:S(2)}) async-start(), calls=%async_computation | async-start | bytes 2097152 | tf_op jit(solution)/shard_map/psum | solution.py:21
  10.8 6.5 copy-start.5
  10.8 776.9 %all-reduce.6.cloned.1.call-start = ((), (), s32[]{:S(2)}) async-start(), calls=%async_computation.1 | async-start | bytes 16777216
  17.2 44.7 %copy-start = (f32[32,8192]{1,0:T(8,128)S(1)}, f32[32,8192]{1,0:T(8,128)}, u32[]{:S(2)}) copy-start(f32[32,8192]{1,0:T(8,128)} %param.7) | copy-start | bytes 3145732
  17.2 44.7 %copy-start.1 = (f32[32,8192]{1,0:T(8,128)S(1)}, f32[32,8192]{1,0:T(8,128)}, u32[]{:S(2)}) copy-start(f32[32,8192]{1,0:T(8,128)} %param.9) | copy-start | bytes 3145732
  17.2 770.5 %copy-start.2 = (f32[1,4,8192]{2,1,0:T(4,128)S(1)}, f32[1,4,8192]{2,1,0:T(4,128)}, u32[]{:S(2)}) copy-start(f32[1,4,8192]{2,1,0:T(4,128)} %param.11) | copy-start | bytes 393220
  17.2 770.5 %copy-start.3 = (f32[1,4,8192]{2,1,0:T(4,128)S(1)}, f32[1,4,8192]{2,1,0:T(4,128)}, u32[]{:S(2)}) copy-start(f32[1,4,8192]{2,1,0:T(4,128)} %param.12) | copy-start | bytes 393220
  17.2 770.5 %copy-start.4 = (f32[1,4,8192]{2,1,0:T(4,128)S(1)}, f32[1,4,8192]{2,1,0:T(4,128)}, u32[]{:S(2)}) copy-start(f32[1,4,8192]{2,1,0:T(4,128)} %param.13) | copy-start | bytes 393220
Sparse Core Ops, SparseCore 0:
  11.2 49.2 all-reduce.3
  63.4 724.2 all-reduce.5
where the time goes:
time: 803 us; the launch traced here: 796 us
  waiting for transfers between devices  766 us (95%)
  other arithmetic  15.1 us (2%)
  between operations  14.9 us (2%)
    unnamed x3, waiting for transfers between devices  724 us
    psum x1, waiting for transfers between devices, on_device(): total = lax.psum(decoded, 'replica')  41.9 us
  transfers between devices with their start and end apart: 2, of which 2 were waited for; matrix products, arithmetic and copies ran while one was open for 1% of the time, Pallas kernels for 0%

commit v1 on v0

--- a/solution.py
+++ b/solution.py
@@ -5,26 +5,123 @@
 
 BLOCK = 128
 STEP = 8
+NZ, NY, NH = 8, 4, 2
+F32, F16, BF16 = jnp.float32, jnp.float16, jnp.bfloat16
+COLS_Y, COLS_H, COLS_Z = 2816, 2816, 2560
+FRAG_SCALE = 2048.0
+
+
+def place(z, y, h):
+    return ((z % NZ) * NY + y % NY) * NH + h % NH
+
+
+def perm_of(step):
+    return [
+        (place(z, y, h), place(*step(z, y, h)))
+        for z in range(NZ)
+        for y in range(NY)
+        for h in range(NH)
+    ]
+
+
+def along_y(x, k):
+    return lax.ppermute(x, "fsdp", perm_of(lambda z, y, h: (z, y + k, h)))
+
+
+def along_h(x):
+    return lax.ppermute(x, "fsdp", perm_of(lambda z, y, h: (z, y, h + 1)))
+
+
+def along_z(x, k):
+    return lax.ppermute(x, "fsdp", perm_of(lambda z, y, h: (z + k, y, h)))
+
+
+def pair_z(x, shift):
+    return lax.ppermute(
+        x, "fsdp", perm_of(lambda z, y, h: ((((z + shift) % NZ) ^ 1) - shift, y, h))
+    )
+
+
+def take(x, index, axis):
+    return lax.dynamic_index_in_dim(x, index, axis, keepdims=False)
+
+
+def rows_of(x, h, axis):
+    low = lax.slice_in_dim(x, 0, 4, axis=axis)
+    high = lax.slice_in_dim(x, 4, 8, axis=axis)
+    return jnp.where(h == 0, low, high)
+
+
+def direct(x, me, size, axis, send, factor):
+    parts = [
+        send(take(x, lax.rem(me + k, size), axis).astype(F16), k) for k in range(1, size)
+    ]
+    total = take(x, me, axis).astype(F32)
+    for part in parts:
+        total = total + part.astype(F32)
+    return total * factor
+
+
+def bucket_sum(g, f):
+    z, y, h = f // (NY * NH), (f // NH) % NY, f % NH
+    p, j = z % 2, z // 2
+    g = g.reshape(NZ, NY, 8, g.shape[-1])
+    ga = g[..., :COLS_Y]
+    gc = g[..., COLS_Y : COLS_Y + COLS_H]
+    gb = g[..., COLS_Y + COLS_H :].reshape(NZ // 2, 2, NY, 8, COLS_Z)
+    c_part = along_h(rows_of(gc, 1 - h, 2))
+    b_part = pair_z(take(gb, 1 - p, 1), 0)
+    a_parts = [along_y(take(ga, lax.rem(y + k, NY), 1), k) for k in range(1, NY)]
+    a = take(ga, y, 1).astype(F32)
+    for part in a_parts:
+        a = a + part.astype(F32)
+    a = (a * 16.0).reshape(NZ // 2, 2, 8, COLS_Y)
+    c = (rows_of(gc, h, 2).astype(F32) + c_part.astype(F32)) * 32.0
+    b = (take(gb, p, 1).astype(F32) + b_part.astype(F32)) * 32.0
+    a_part = pair_z(take(a, 1 - p, 1).astype(F16), 0)
+    b_part = along_h(rows_of(b, 1 - h, 2).astype(F16))
+    a = (take(a, p, 1) + a_part.astype(F32)) * 0.5
+    b = (rows_of(b, h, 2) + b_part.astype(F32)) * 0.5
+    c = direct(c, y, NY, 1, along_y, 0.25).reshape(NZ // 2, 2, 4, COLS_H)
+    a_part = along_h(rows_of(a, 1 - h, 1).astype(F16))
+    c_part = pair_z(take(c, 1 - p, 1).astype(F16), 0)
+    a = (rows_of(a, h, 1) + a_part.astype(F32)) * 0.5
+    c = (take(c, p, 1) + c_part.astype(F32)) * 0.5
+    b = direct(b, y, NY, 1, along_y, 0.25)
+    ac = jnp.concatenate([a, c], axis=-1)
+    t = jnp.concatenate([ac, b], axis=-1)
+    return direct(t, j, NZ // 2, 0, lambda x, k: along_z(x, 2 * k), 0.25)
+
+
+def fragment_total(delta, r):
+    rows, width = delta.shape
+    blocks = delta.reshape(rows, width // BLOCK, BLOCK)
+    amax = jnp.max(jnp.abs(blocks), axis=-1)
+    scale = ((amax + 1e-06) / 448.0).astype(BF16).astype(F32)[..., None]
+    encoded = (blocks / scale).astype(BF16)
+    decoded = (encoded.astype(F32) * scale).reshape(2, rows // 2, width)
+    core = r % 2
+    swap_core = [(0, 1), (1, 0), (2, 3), (3, 2)]
+    swap_chip = [(0, 2), (2, 0), (1, 3), (3, 1)]
+    other = lax.ppermute(take(decoded, 1 - core, 0), "replica", swap_core)
+    pair = ((take(decoded, core, 0) + other) * FRAG_SCALE).astype(F16)
+    far = lax.ppermute(pair, "replica", swap_chip)
+    mine = (pair.astype(F32) + far.astype(F32)) * (1.0 / FRAG_SCALE)
+    theirs = lax.ppermute(mine, "replica", swap_core)
+    low = jnp.where(core == 0, mine, theirs)
+    high = jnp.where(core == 0, theirs, mine)
+    return jnp.concatenate([low, high], axis=0)
 
 
 def on_device(global_frag, local_frag, outer_mom, grads, inner_param, inner_m, inner_v):
-    frag_rows = global_frag.shape[0]
-    width = global_frag.shape[1]
+    f = lax.axis_index("fsdp")
+    r = lax.axis_index("replica")
     groups = lax.axis_size("fsdp")
-    local_grad = grads[0, 0]
-    delta = global_frag - local_frag[0]
-    blocks = delta.reshape(frag_rows, width // BLOCK, BLOCK)
-    amax = jnp.max(jnp.abs(blocks), axis=-1)
-    scale = ((amax + 1e-06) / 448.0).astype(jnp.bfloat16)
-    encoded = (blocks / scale.astype(jnp.float32)[..., None]).astype(jnp.bfloat16)
-    decoded = encoded.astype(jnp.float32) * scale.astype(jnp.float32)[..., None]
-    total = lax.psum(decoded, "replica")
-    average = (0.25 * total).reshape(frag_rows, width)
+    summed = bucket_sum(grads[0, 0], f)
+    total = fragment_total(global_frag - local_frag[0], r)
+    average = 0.25 * total
     new_mom = 0.9 * outer_mom + average
     new_global = global_frag - 0.7 * (average + 0.9 * new_mom)
-    summed = lax.psum_scatter(
-        local_grad.astype(jnp.float32), "fsdp", scatter_dimension=0, tiled=True
-    )
     gmean = (summed / groups)[None]
     new_m = 0.9 * inner_m + 0.1 * gmean
     new_v = 0.95 * inner_v + 0.05 * gmean * gmean

time: 803 us -> 88.6 us (0.11)
  waiting for transfers between devices: 766 us -> 29.6 us
  starting transfers between devices: 0.08 us -> 34.1 us
  between operations: 14.9 us -> 1.15 us
    unnamed x3 -> x0, waiting for transfers between devices: 724 us -> none
    psum x1 -> x0, waiting for transfers between devices: 41.9 us -> none  [on_device(): total = lax.psum(decoded, 'replica')]
    ppermute x0 -> x21, starting transfers between devices: none -> 34.1 us  [the longest x9 11.3 us: along_y(): return lax.ppermute(x, 'fsdp', perm_of(lambda z, y, h: (z, y + k, h)))]
    ppermute x0 -> x21, waiting for transfers between devices: none -> 29.6 us  [the longest x9 9.36 us: along_y(): return lax.ppermute(x, 'fsdp', perm_of(lambda z, y, h: (z, y + k, h)))]
  transfers between devices with their start and end apart: 2 -> 21, of which waited for: 2 -> 10; matrix products, arithmetic and copies ran while one was open for 1% -> 21% of each run, Pallas kernels for 0% -> 0%
where the time goes in v1:
time: 88.6 us; the launch traced here: 87.4 us
  starting transfers between devices  34.1 us (38%)
  waiting for transfers between devices  29.6 us (33%)
  other arithmetic  15.9 us (18%)
  local copies, waits for them, and re-layouts  6.54 us (7%)
  between operations  1.15 us (1%)
    ppermute x9, starting transfers between devices, along_y(): return lax.ppermute(x, 'fsdp', perm_of(lambda z, y, h: (z, y + k, h)))  11.3 us
    ppermute x3, starting transfers between devices, along_z(): return lax.ppermute(x, 'fsdp', perm_of(lambda z, y, h: (z + k, y, h)))  11.1 us
    ppermute x9, waiting for transfers between devices, along_y(): return lax.ppermute(x, 'fsdp', perm_of(lambda z, y, h: (z, y + k, h)))  9.36 us
    ppermute x3, waiting for transfers between devices, pair_z(): lax.ppermute(x, 'fsdp', perm_of(lambda z, y, h: (((z + shift) % NZ ^ 1) -...  8.92 us
    ppermute x3, waiting for transfers between devices, along_h(): return lax.ppermute(x, 'fsdp', perm_of(lambda z, y, h: (z, y, h + 1)))  8.58 us
    ppermute x3, starting transfers between devices, pair_z(): lax.ppermute(x, 'fsdp', perm_of(lambda z, y, h: (((z + shift) % NZ ^ 1) -...  5.58 us
    ppermute x3, starting transfers between devices, along_h(): return lax.ppermute(x, 'fsdp', perm_of(lambda z, y, h: (z, y, h + 1)))  4.43 us
    select_n x1, other arithmetic, rows_of(): return jnp.where(h == 0, low, high)  3.25 us
  transfers between devices with their start and end apart: 21, of which 10 were waited for; matrix products, arithmetic and copies ran while one was open for 21% of the time, Pallas kernels for 0%

profile of v1, /device:TPU:24, one launch (start us, length us, event | category | flops | bytes accessed | tf_op | source)
XLA Modules:
  0.0 87.4 jit_solution(14543079670830767144)
XLA Ops:
  0.7 1.5 %slice.41 = bf16[8,4,8,2816]{3,2,1,0:T(8,128)(2,1)S(1)} slice(bf16[8,4,8,8192]{3,2,1,0:T(8,128)(2,1)} %bitcast.112), slice={[0:8], [0:4], [0:8], [0:2816]} | slice | bytes 2883584 | tf_op jit(solution)/shard_map/slice | solution.py:69
  2.2 1.0 %dynamic-slice_bitcast_fusion.3 = (bf16[8,8,2816]{2,1,0:T(8,128)(2,1)}, bf16[8,8,2816]{2,1,0:T(8,128)(2,1)}, bf16[8,8,2816]{2,1,0:T(8,128)(2,1)}) fusion(bf16[8,4,8,2816]{3,2,1,0:T(8,128)(2,1)S(1)} %slice.41, s32[]{:T(128)S(6)} %select_n.150, s32[]{:T(128)S(6)} %select_n.152, s32[]{:T(128)S(6)} %select_n.151), kind=kLoop, calls=%fused_computation.37 | loop fusion | bytes 2162700 | tf_op jit(solution)/shard_map/jit(dynamic_index_in_dim)/squeeze | solution.py:46
  3.2 2.0 %collective-permute-start.3 = (bf16[8,8,2816]{2,1,0:T(8,128)(2,1)}, bf16[8,8,2816]{2,1,0:T(8,128)(2,1)}, u32[]{:S(2)}, u32[]{:S(2)}) collective-permute-start(bf16[8,8,2816]{2,1,0:T(8,128)(2,1)} %get-tuple-element.12), channel_id=1, source_target_pairs={{0,2},{1,3},{2,4},{3,5},{4,6},{5,7},{6,0},{7,1},{8,10},{9,11},{10,... | collective-permute-start | bytes 1081352 | tf_op jit(solution)/shard_map/ppermute | solution.py:28
  5.1 0.9 collective-permute-start.4
  6.0 3.2 %broadcast_select_fusion = bf16[8,4,4,2816]{3,2,1,0:T(4,128)(2,1)} fusion(pred[]{:T(512)S(6)} %eq.21, bf16[8,4,8,8192]{3,2,1,0:T(8,128)(2,1)} %bitcast.113), kind=kLoop, calls=%fused_computation.14 | loop fusion | flops 360448 | bytes 2162689 | tf_op jit(solution)/shard_map/jit(_where)/select_n | solution.py:52
  9.3 3.0 %collective-permute-start.8 = (bf16[8,4,4,2816]{3,2,1,0:T(4,128)(2,1)}, bf16[8,4,4,2816]{3,2,1,0:T(4,128)(2,1)}, u32[]{:S(2)}, u32[]{:S(2)}) collective-permute-start(bf16[8,4,4,2816]{3,2,1,0:T(4,128)(2,1)} %broadcast_select_fusion), channel_id=1, source_target_pairs={{0,1},{1,0},{2,3},{3,2},{4,5},{5,4},{6,7},{7,6},{8,9},{9,8},{10,11... | collective-permute-start | bytes 2162696 | tf_op jit(solution)/shard_map/ppermute | solution.py:32
  12.3 1.4 %slice.46 = bf16[8,4,8,2560]{3,2,1,0:T(8,128)(2,1)S(1)} slice(bf16[8,4,8,8192]{3,2,1,0:T(8,128)(2,1)} %bitcast.114), slice={[0:8], [0:4], [0:8], [5632:8192]} | slice | bytes 2621440 | tf_op jit(solution)/shard_map/slice | solution.py:71
  13.8 1.0 %constant_dynamic-slice_fusion.1 = (bf16[4,1,4,8,2560]{4,3,2,1,0:T(8,128)(2,1)}, bf16[4,1,4,8,2560]{4,3,2,1,0:T(8,128)(2,1)S(1)}) fusion(bf16[4,2,4,8,2560]{4,3,2,1,0:T(8,128)(2,1)S(1)} %bitcast.116, s32[]{:T(128)S(6)} %select_n.155, s32[]{:T(128)S(6)} %select_n.156), kind=kLoop, calls=%fused_computation.75 | loop fusion | bytes 2621448 | tf_op jit(solution)/shard_map/jit(dynamic_index_in_dim)/dynamic_slice | solution.py:46
  14.7 0.9 %copy.32 = bf16[4,1,4,8,2560]{4,3,0,2,1:T(8,128)(2,1)} copy(bf16[4,1,4,8,2560]{4,3,2,1,0:T(8,128)(2,1)S(1)} %get-tuple-element.19) | data formatting | bytes 1310720 | tf_op jit(solution)/shard_map/jit(dynamic_index_in_dim)/dynamic_slice | solution.py:46
  15.6 1.9 %collective-permute-start.13 = (bf16[4,4,8,2560]{3,2,0,1:T(8,128)(2,1)}, bf16[4,4,8,2560]{3,2,0,1:T(8,128)(2,1)}, u32[]{:S(2)}, u32[]{:S(2)}) collective-permute-start(bf16[4,4,8,2560]{3,2,0,1:T(8,128)(2,1)} %bitcast.111), channel_id=1, source_target_pairs={{0,8},{1,9},{2,10},{3,11},{4,12},{5,13},{6,14},{7,15},{8,0},{9,1},... | collective-permute-start | bytes 1966088 | tf_op jit(solution)/shard_map/ppermute | solution.py:40
  17.5 1.1 %abs_bitcast_fusion = (f32[4,8,64,128]{3,1,2,0:T(8,128)S(1)}, f32[32,8192]{1,0:T(8,128)}) fusion(f32[32,8192]{1,0:T(8,128)S(1)} %copy-done, f32[1,32,8192]{2,1,0:T(8,128)S(1)} %copy-done.4), kind=kLoop, calls=%fused_computation.9 | loop fusion | flops 524288 | bytes 4194304
  18.6 0.2 copy.27
  18.8 0.3 reduce_max.9
  19.2 0.3 div.62
  19.5 0.2 div.63
  19.7 1.4 %convert_multiply_fusion = f32[2,16,8192]{2,1,0:T(8,128)S(1)} fusion(f32[2,16,8192]{2,1,0:T(8,128)S(1)} %div.63, f32[2,16,8192]{2,1,0:T(8,128)} %bitcast.117), kind=kLoop, calls=%fused_computation.7 | loop fusion | flops 1048576 | bytes 3145728 | tf_op jit(solution)/shard_map/mul | solution.py:102
  21.1 1.8 %collective-permute-done.5 = bf16[8,8,2816]{2,1,0:T(8,128)(2,1)} collective-permute-done((bf16[8,8,2816]{2,1,0:T(8,128)(2,1)}, bf16[8,8,2816]{2,1,0:T(8,128)(2,1)}, u32[]{:S(2)}, u32[]{:S(2)}) %collective-permute-start.5) | collective-permute-done | bytes 360480 | tf_op jit(solution)/shard_map/ppermute | solution.py:28
  22.9 1.4 %fusion.3 = f32[8,8,2816]{2,1,0:T(8,128)S(1)} fusion(bf16[8,8,2816]{2,1,0:T(8,128)(2,1)} %collective-permute-done.5, bf16[8,8,2816]{2,1,0:T(8,128)(2,1)} %collective-permute-done.4, bf16[8,8,2816]{2,1,0:T(8,128)(2,1)} %collective-permute-done.3, bf16[8,4,8,2816]{3,2,1,0:T(8,128)(2,1)S(1)} %slice.41, s32[]{:T(128)S(6)} %select_n.149), kind=kLoop, calls=%fused_computation.13 | loop fusion | flops 1441792 | bytes 2162692 | tf_op jit(solution)/shard_map/mul | solution.py:78
  24.3 2.0 %collective-permute-start.6 = (f16[4,8,2816]{2,1,0:T(8,128)(2,1)S(1)}, f16[4,8,2816]{2,1,0:T(8,128)(2,1)S(1)}, u32[]{:S(2)}, u32[]{:S(2)}) collective-permute-start(f16[4,8,2816]{2,1,0:T(8,128)(2,1)S(1)} %fusion.10), channel_id=1, source_target_pairs={{0,8},{1,9},{2,10},{3,11},{4,12},{5,13},{6,14},{7,15},{8,0},{9,1},... | collective-permute-start | bytes 540680 | tf_op jit(solution)/shard_map/ppermute | solution.py:40
  26.6 8.9 %collective-permute-done.6 = f16[4,8,2816]{2,1,0:T(8,128)(2,1)S(1)} collective-permute-done((f16[4,8,2816]{2,1,0:T(8,128)(2,1)S(1)}, f16[4,8,2816]{2,1,0:T(8,128)(2,1)S(1)}, u32[]{:S(2)}, u32[]{:S(2)}) %collective-permute-start.6) | collective-permute-done | bytes 180256 | tf_op jit(solution)/shard_map/ppermute | solution.py:40
  35.6 0.6 collective-permute-start.7
  36.3 1.6 %collective-permute-start.1 = (f16[16,8192]{1,0:T(8,128)(2,1)S(1)}, f16[16,8192]{1,0:T(8,128)(2,1)S(1)}, u32[]{:S(2)}, u32[]{:S(2)}) collective-permute-start(f16[16,8192]{1,0:T(8,128)(2,1)S(1)} %fusion.5), channel_id=1, source_target_pairs={{0,128},{128,0},{64,192},{192,64},{1,129},{129,1},{65,193},{193,65... | collective-permute-start | bytes 786440 | tf_op jit(solution)/shard_map/ppermute | solution.py:108
  37.8 4.9 %collective-permute-done.7 = f16[4,4,2816]{2,1,0:T(4,128)(2,1)S(1)} collective-permute-done((f16[4,4,2816]{2,1,0:T(4,128)(2,1)S(1)}, f16[4,4,2816]{2,1,0:T(4,128)(2,1)S(1)}, u32[]{:S(2)}, u32[]{:S(2)}) %collective-permute-start.7) | collective-permute-done | bytes 90144 | tf_op jit(solution)/shard_map/ppermute | solution.py:32
  42.9 1.3 %fusion = f32[4,4,8,2560]{3,2,0,1:T(8,128)S(1)} fusion(bf16[4,4,8,2560]{3,2,0,1:T(8,128)(2,1)} %collective-permute-done.13, bf16[4,1,4,8,2560]{4,3,2,1,0:T(8,128)(2,1)S(1)} %copy-done.2), kind=kLoop, calls=%fused_computation.2 | loop fusion | flops 1310720 | bytes 2621440 | tf_op jit(solution)/shard_map/mul | solution.py:80
  44.1 2.8 %add_multiply_fusion = f32[8,4,4,2816]{3,2,1,0:T(4,128)S(1)} fusion(bf16[8,4,4,2816]{3,2,1,0:T(4,128)(2,1)} %collective-permute-done.8, pred[]{:T(512)S(6)} %eq.20, bf16[8,4,8,8192]{3,2,1,0:T(8,128)(2,1)} %bitcast.115), kind=kLoop, calls=%fused_computation | loop fusion | flops 1802240 | bytes 3604481 | tf_op jit(solution)/shard_map/mul | solution.py:79
  46.9 0.2 fusion.12
  47.1 3.1 %collective-permute-start.10 = (f16[8,4,2816]{2,1,0:T(4,128)(2,1)S(1)}, f16[8,4,2816]{2,1,0:T(4,128)(2,1)S(1)}, u32[]{:S(2)}, u32[]{:S(2)}) collective-permute-start(f16[8,4,2816]{2,1,0:T(4,128)(2,1)S(1)} %get-tuple-element.17), channel_id=1, source_target_pairs={{0,4},{1,5},{2,6},{3,7},{4,0},{5,1},{6,2},{7,3},{8,12},{9,13},{10,... | collective-permute-start | bytes 540680 | tf_op jit(solution)/shard_map/ppermute | solution.py:28
  50.2 0.7 collective-permute-start.11
  51.0 2.5 %collective-permute-start.9 = (f16[8,4,2816]{2,1,0:T(4,128)(2,1)S(1)}, f16[8,4,2816]{2,1,0:T(4,128)(2,1)S(1)}, u32[]{:S(2)}, u32[]{:S(2)}) collective-permute-start(f16[8,4,2816]{2,1,0:T(4,128)(2,1)S(1)} %get-tuple-element.15), channel_id=1, source_target_pairs={{0,2},{1,3},{2,4},{3,5},{4,6},{5,7},{6,0},{7,1},{8,10},{9,11},{10,... | collective-permute-start | bytes 540680 | tf_op jit(solution)/shard_map/ppermute | solution.py:28
  53.4 0.2 select_convert_fusion
  53.7 0.8 collective-permute-start.14
  54.5 2.4 %collective-permute-done.11 = f16[8,4,2816]{2,1,0:T(4,128)(2,1)S(1)} collective-permute-done((f16[8,4,2816]{2,1,0:T(4,128)(2,1)S(1)}, f16[8,4,2816]{2,1,0:T(4,128)(2,1)S(1)}, u32[]{:S(2)}, u32[]{:S(2)}) %collective-permute-start.11) | collective-permute-done | bytes 180256 | tf_op jit(solution)/shard_map/ppermute | solution.py:28
  56.9 0.2 fusion.8
  57.2 1.7 %collective-permute-start.12 = (f16[4,4,2816]{2,1,0:T(4,128)(2,1)S(1)}, f16[4,4,2816]{2,1,0:T(4,128)(2,1)S(1)}, u32[]{:S(2)}, u32[]{:S(2)}) collective-permute-start(f16[4,4,2816]{2,1,0:T(4,128)(2,1)S(1)} %fusion.20), channel_id=1, source_target_pairs={{0,8},{1,9},{2,10},{3,11},{4,12},{5,13},{6,14},{7,15},{8,0},{9,1},... | collective-permute-start | bytes 270344 | tf_op jit(solution)/shard_map/ppermute | solution.py:40
  58.8 3.7 %collective-permute-done.14 = f16[4,4,4,2560]{3,2,0,1:T(4,128)(2,1)S(1)} collective-permute-done((f16[4,4,4,2560]{3,2,0,1:T(4,128)(2,1)S(1)}, f16[4,4,4,2560]{3,2,0,1:T(4,128)(2,1)S(1)}, u32[]{:S(2)}, u32[]{:S(2)}) %collective-permute-start.14) | collective-permute-done | bytes 327712 | tf_op jit(solution)/shard_map/ppermute | solution.py:32
  62.5 0.3 add_multiply_fusion.1
  63.0 1.6 %collective-permute-start.16 = (f16[4,4,2560]{2,1,0:T(4,128)(2,1)S(1)}, f16[4,4,2560]{2,1,0:T(4,128)(2,1)S(1)}, u32[]{:S(2)}, u32[]{:S(2)}) collective-permute-start(f16[4,4,2560]{2,1,0:T(4,128)(2,1)S(1)} %get-tuple-element.24), channel_id=1, source_target_pairs={{0,4},{1,5},{2,6},{3,7},{4,0},{5,1},{6,2},{7,3},{8,12},{9,13},{10,... | collective-permute-start | bytes 245768 | tf_op jit(solution)/shard_map/ppermute | solution.py:28
  64.6 0.4 collective-permute-start.17
  65.1 2.3 %collective-permute-done.15 = f16[4,4,2560]{2,1,0:T(4,128)(2,1)S(1)} collective-permute-done((f16[4,4,2560]{2,1,0:T(4,128)(2,1)S(1)}, f16[4,4,2560]{2,1,0:T(4,128)(2,1)S(1)}, u32[]{:S(2)}, u32[]{:S(2)}) %collective-permute-start.15) | collective-permute-done | bytes 81952 | tf_op jit(solution)/shard_map/ppermute | solution.py:28
  67.4 1.6 %collective-permute-done.16 = f16[4,4,2560]{2,1,0:T(4,128)(2,1)S(1)} collective-permute-done((f16[4,4,2560]{2,1,0:T(4,128)(2,1)S(1)}, f16[4,4,2560]{2,1,0:T(4,128)(2,1)S(1)}, u32[]{:S(2)}, u32[]{:S(2)}) %collective-permute-start.16) | collective-permute-done | bytes 81952 | tf_op jit(solution)/shard_map/ppermute | solution.py:28
  69.0 1.2 %collective-permute-done.17 = f16[4,4,2560]{2,1,0:T(4,128)(2,1)S(1)} collective-permute-done((f16[4,4,2560]{2,1,0:T(4,128)(2,1)S(1)}, f16[4,4,2560]{2,1,0:T(4,128)(2,1)S(1)}, u32[]{:S(2)}, u32[]{:S(2)}) %collective-permute-start.17) | collective-permute-done | bytes 81952 | tf_op jit(solution)/shard_map/ppermute | solution.py:28
  70.6 3.3 %collective-permute-start.18 = (f16[4,8192]{1,0:T(4,128)(2,1)S(1)}, f16[4,8192]{1,0:T(4,128)(2,1)S(1)}, u32[]{:S(2)}, u32[]{:S(2)}) collective-permute-start(f16[4,8192]{1,0:T(4,128)(2,1)S(1)} %get-tuple-element.25), channel_id=1, source_target_pairs={{0,16},{1,17},{2,18},{3,19},{4,20},{5,21},{6,22},{7,23},{8,24},{9,... | collective-permute-start | bytes 196616 | tf_op jit(solution)/shard_map/ppermute | solution.py:36
  73.9 5.0 %collective-permute-start.19 = (f16[4,8192]{1,0:T(4,128)(2,1)S(1)}, f16[4,8192]{1,0:T(4,128)(2,1)S(1)}, u32[]{:S(2)}, u32[]{:S(2)}) collective-permute-start(f16[4,8192]{1,0:T(4,128)(2,1)S(1)} %get-tuple-element.27), channel_id=1, source_target_pairs={{0,32},{1,33},{2,34},{3,35},{4,36},{5,37},{6,38},{7,39},{8,40},{9,... | collective-permute-start | bytes 196616 | tf_op jit(solution)/shard_map/ppermute | solution.py:36
  79.0 2.7 %collective-permute-start.20 = (f16[4,8192]{1,0:T(4,128)(2,1)S(1)}, f16[4,8192]{1,0:T(4,128)(2,1)S(1)}, u32[]{:S(2)}, u32[]{:S(2)}) collective-permute-start(f16[4,8192]{1,0:T(4,128)(2,1)S(1)} %get-tuple-element.26), channel_id=1, source_target_pairs={{0,48},{1,49},{2,50},{3,51},{4,52},{5,53},{6,54},{7,55},{8,56},{9,... | collective-permute-start | bytes 196616 | tf_op jit(solution)/shard_map/ppermute | solution.py:36
  81.8 0.3 collective-permute-done.19
  82.1 2.5 %collective-permute-done.20 = f16[4,8192]{1,0:T(4,128)(2,1)S(1)} collective-permute-done((f16[4,8192]{1,0:T(4,128)(2,1)S(1)}, f16[4,8192]{1,0:T(4,128)(2,1)S(1)}, u32[]{:S(2)}, u32[]{:S(2)}) %collective-permute-start.20) | collective-permute-done | bytes 65568 | tf_op jit(solution)/shard_map/ppermute | solution.py:36
  84.6 1.0 %multiply_subtract_fusion.1 = (f32[1,4,8192]{2,1,0:T(4,128)}, f32[1,4,8192]{2,1,0:T(4,128)}, f32[1,4,8192]{2,1,0:T(4,128)}) fusion(f32[1,4,8192]{2,1,0:T(4,128)S(1)} %copy-done.5, f16[4,8192]{1,0:T(4,128)(2,1)S(1)} %collective-permute-done.20, f16[4,8192]{1,0:T(4,128)(2,1)S(1)} %collective-permute-done.19, f16[4,8192]{1,0:T(4,128)(2,1)S(1)} %collective-permute-done.18, ...), kind=kLoop, calls=%fused_computation.61 | loop fusion | flops 720896 | bytes 1114116 | tf_op jit(solution)/shard_map/sub | solution.py:130
  85.8 1.6 %multiply_subtract_fusion = (f32[32,8192]{1,0:T(8,128)}, f32[32,8192]{1,0:T(8,128)}) fusion(f32[32,8192]{1,0:T(8,128)S(1)} %copy-done.1, f32[16,8192]{1,0:T(8,128)S(1)} %get-tuple-element.21, f32[16,8192]{1,0:T(8,128)S(1)} %get-tuple-element.20, f32[32,8192]{1,0:T(8,128)S(1)} %copy-done.3), kind=kLoop, calls=%fused_computation.5 | loop fusion | flops 2097152 | bytes 5242880 | tf_op jit(solution)/shard_map/sub | solution.py:124
  (46 shorter events, 1.4 us)
Async XLA Ops:
  3.2 17.9 %collective-permute-start.3 = (bf16[8,8,2816]{2,1,0:T(8,128)(2,1)}, bf16[8,8,2816]{2,1,0:T(8,128)(2,1)}, u32[]{:S(2)}, u32[]{:S(2)}) collective-permute-start(bf16[8,8,2816]{2,1,0:T(8,128)(2,1)} %get-tuple-element.12), channel_id=1, source_target_pairs={{0,2},{1,3},{2,4},{3,5},{4,6},{5,7},{6,0},{7,1},{8,10},{9,11},{10,... | collective-permute-start | bytes 1081352 | tf_op jit(solution)/shard_map/ppermute | solution.py:28
  5.1 16.0 %collective-permute-start.4 = (bf16[8,8,2816]{2,1,0:T(8,128)(2,1)}, bf16[8,8,2816]{2,1,0:T(8,128)(2,1)}, u32[]{:S(2)}, u32[]{:S(2)}) collective-permute-start(bf16[8,8,2816]{2,1,0:T(8,128)(2,1)} %get-tuple-element.14), channel_id=1, source_target_pairs={{0,4},{1,5},{2,6},{3,7},{4,0},{5,1},{6,2},{7,3},{8,12},{9,13},{10,... | collective-permute-start | bytes 1081352 | tf_op jit(solution)/shard_map/ppermute | solution.py:28
  6.0 16.9 %collective-permute-start.5 = (bf16[8,8,2816]{2,1,0:T(8,128)(2,1)}, bf16[8,8,2816]{2,1,0:T(8,128)(2,1)}, u32[]{:S(2)}, u32[]{:S(2)}) collective-permute-start(bf16[8,8,2816]{2,1,0:T(8,128)(2,1)} %get-tuple-element.13), channel_id=1, source_target_pairs={{0,6},{1,7},{2,0},{3,1},{4,2},{5,3},{6,4},{7,5},{8,14},{9,15},{10,... | collective-permute-start | bytes 1081352 | tf_op jit(solution)/shard_map/ppermute | solution.py:28
  9.3 34.9 %collective-permute-start.8 = (bf16[8,4,4,2816]{3,2,1,0:T(4,128)(2,1)}, bf16[8,4,4,2816]{3,2,1,0:T(4,128)(2,1)}, u32[]{:S(2)}, u32[]{:S(2)}) collective-permute-start(bf16[8,4,4,2816]{3,2,1,0:T(4,128)(2,1)} %broadcast_select_fusion), channel_id=1, source_target_pairs={{0,1},{1,0},{2,3},{3,2},{4,5},{5,4},{6,7},{7,6},{8,9},{9,8},{10,11... | collective-permute-start | bytes 2162696 | tf_op jit(solution)/shard_map/ppermute | solution.py:32
  13.7 3.8 %copy-start = (f32[32,8192]{1,0:T(8,128)S(1)}, f32[32,8192]{1,0:T(8,128)}, u32[]{:S(2)}) copy-start(f32[32,8192]{1,0:T(8,128)} %param.7) | copy-start | bytes 3145732
  13.7 3.8 %copy-start.4 = (f32[1,32,8192]{2,1,0:T(8,128)S(1)}, f32[1,32,8192]{2,1,0:T(8,128)}, u32[]{:S(2)}) copy-start(f32[1,32,8192]{2,1,0:T(8,128)} %param.8) | copy-start | bytes 3145732
  15.6 27.2 %collective-permute-start.13 = (bf16[4,4,8,2560]{3,2,0,1:T(8,128)(2,1)}, bf16[4,4,8,2560]{3,2,0,1:T(8,128)(2,1)}, u32[]{:S(2)}, u32[]{:S(2)}) collective-permute-start(bf16[4,4,8,2560]{3,2,0,1:T(8,128)(2,1)} %bitcast.111), channel_id=1, source_target_pairs={{0,8},{1,9},{2,10},{3,11},{4,12},{5,13},{6,14},{7,15},{8,0},{9,1},... | collective-permute-start | bytes 1966088 | tf_op jit(solution)/shard_map/ppermute | solution.py:40
  24.3 11.1 %collective-permute-start.6 = (f16[4,8,2816]{2,1,0:T(8,128)(2,1)S(1)}, f16[4,8,2816]{2,1,0:T(8,128)(2,1)S(1)}, u32[]{:S(2)}, u32[]{:S(2)}) collective-permute-start(f16[4,8,2816]{2,1,0:T(8,128)(2,1)S(1)} %fusion.10), channel_id=1, source_target_pairs={{0,8},{1,9},{2,10},{3,11},{4,12},{5,13},{6,14},{7,15},{8,0},{9,1},... | collective-permute-start | bytes 540680 | tf_op jit(solution)/shard_map/ppermute | solution.py:40
  26.4 9.8 %collective-permute-start = (f32[16,8192]{1,0:T(8,128)S(1)}, f32[16,8192]{1,0:T(8,128)S(1)}, u32[]{:S(2)}, u32[]{:S(2)}) collective-permute-start(f32[16,8192]{1,0:T(8,128)S(1)} %dynamic-slice_bitcast_fusion), channel_id=1, source_target_pairs={{0,64},{64,0},{128,192},{192,128},{1,65},{65,1},{129,193},{193,129... | collective-permute-start | bytes 1572872 | tf_op jit(solution)/shard_map/ppermute | solution.py:106
  26.6 16.3 %copy-start.2 = (bf16[4,1,4,8,2560]{4,3,2,1,0:T(8,128)(2,1)S(1)}, bf16[4,1,4,8,2560]{4,3,2,1,0:T(8,128)(2,1)}, u32[]{:S(2)}) copy-start(bf16[4,1,4,8,2560]{4,3,2,1,0:T(8,128)(2,1)} %get-tuple-element.18) | copy-start | bytes 1966084
  35.6 7.2 %collective-permute-start.7 = (f16[4,4,2816]{2,1,0:T(4,128)(2,1)S(1)}, f16[4,4,2816]{2,1,0:T(4,128)(2,1)S(1)}, u32[]{:S(2)}, u32[]{:S(2)}) collective-permute-start(f16[4,4,2816]{2,1,0:T(4,128)(2,1)S(1)} %select_convert_fusion.1), channel_id=1, source_target_pairs={{0,1},{1,0},{2,3},{3,2},{4,5},{5,4},{6,7},{7,6},{8,9},{9,8},{10,11... | collective-permute-start | bytes 270344 | tf_op jit(solution)/shard_map/ppermute | solution.py:32
  36.3 45.4 %collective-permute-start.1 = (f16[16,8192]{1,0:T(8,128)(2,1)S(1)}, f16[16,8192]{1,0:T(8,128)(2,1)S(1)}, u32[]{:S(2)}, u32[]{:S(2)}) collective-permute-start(f16[16,8192]{1,0:T(8,128)(2,1)S(1)} %fusion.5), channel_id=1, source_target_pairs={{0,128},{128,0},{64,192},{192,64},{1,129},{129,1},{65,193},{193,65... | collective-permute-start | bytes 786440 | tf_op jit(solution)/shard_map/ppermute | solution.py:108
  47.1 7.4 %collective-permute-start.10 = (f16[8,4,2816]{2,1,0:T(4,128)(2,1)S(1)}, f16[8,4,2816]{2,1,0:T(4,128)(2,1)S(1)}, u32[]{:S(2)}, u32[]{:S(2)}) collective-permute-start(f16[8,4,2816]{2,1,0:T(4,128)(2,1)S(1)} %get-tuple-element.17), channel_id=1, source_target_pairs={{0,4},{1,5},{2,6},{3,7},{4,0},{5,1},{6,2},{7,3},{8,12},{9,13},{10,... | collective-permute-start | bytes 540680 | tf_op jit(solution)/shard_map/ppermute | solution.py:28
  50.2 6.7 %collective-permute-start.11 = (f16[8,4,2816]{2,1,0:T(4,128)(2,1)S(1)}, f16[8,4,2816]{2,1,0:T(4,128)(2,1)S(1)}, u32[]{:S(2)}, u32[]{:S(2)}) collective-permute-start(f16[8,4,2816]{2,1,0:T(4,128)(2,1)S(1)} %get-tuple-element.16), channel_id=1, source_target_pairs={{0,6},{1,7},{2,0},{3,1},{4,2},{5,3},{6,4},{7,5},{8,14},{9,15},{10,... | collective-permute-start | bytes 540680 | tf_op jit(solution)/shard_map/ppermute | solution.py:28
  51.0 6.0 %collective-permute-start.9 = (f16[8,4,2816]{2,1,0:T(4,128)(2,1)S(1)}, f16[8,4,2816]{2,1,0:T(4,128)(2,1)S(1)}, u32[]{:S(2)}, u32[]{:S(2)}) collective-permute-start(f16[8,4,2816]{2,1,0:T(4,128)(2,1)S(1)} %get-tuple-element.15), channel_id=1, source_target_pairs={{0,2},{1,3},{2,4},{3,5},{4,6},{5,7},{6,0},{7,1},{8,10},{9,11},{10,... | collective-permute-start | bytes 540680 | tf_op jit(solution)/shard_map/ppermute | solution.py:28
  53.7 8.8 %collective-permute-start.14 = (f16[4,4,4,2560]{3,2,0,1:T(4,128)(2,1)S(1)}, f16[4,4,4,2560]{3,2,0,1:T(4,128)(2,1)S(1)}, u32[]{:S(2)}, u32[]{:S(2)}) collective-permute-start(f16[4,4,4,2560]{3,2,0,1:T(4,128)(2,1)S(1)} %select_convert_fusion), channel_id=1, source_target_pairs={{0,1},{1,0},{2,3},{3,2},{4,5},{5,4},{6,7},{7,6},{8,9},{9,8},{10,11... | collective-permute-start | bytes 983048 | tf_op jit(solution)/shard_map/ppermute | solution.py:32
  57.2 7.8 %collective-permute-start.12 = (f16[4,4,2816]{2,1,0:T(4,128)(2,1)S(1)}, f16[4,4,2816]{2,1,0:T(4,128)(2,1)S(1)}, u32[]{:S(2)}, u32[]{:S(2)}) collective-permute-start(f16[4,4,2816]{2,1,0:T(4,128)(2,1)S(1)} %fusion.20), channel_id=1, source_target_pairs={{0,8},{1,9},{2,10},{3,11},{4,12},{5,13},{6,14},{7,15},{8,0},{9,1},... | collective-permute-start | bytes 270344 | tf_op jit(solution)/shard_map/ppermute | solution.py:40
  62.9 4.5 %collective-permute-start.15 = (f16[4,4,2560]{2,1,0:T(4,128)(2,1)S(1)}, f16[4,4,2560]{2,1,0:T(4,128)(2,1)S(1)}, u32[]{:S(2)}, u32[]{:S(2)}) collective-permute-start(f16[4,4,2560]{2,1,0:T(4,128)(2,1)S(1)} %get-tuple-element.22), channel_id=1, source_target_pairs={{0,2},{1,3},{2,4},{3,5},{4,6},{5,7},{6,0},{7,1},{8,10},{9,11},{10,... | collective-permute-start | bytes 245768 | tf_op jit(solution)/shard_map/ppermute | solution.py:28
  63.0 6.0 %collective-permute-start.16 = (f16[4,4,2560]{2,1,0:T(4,128)(2,1)S(1)}, f16[4,4,2560]{2,1,0:T(4,128)(2,1)S(1)}, u32[]{:S(2)}, u32[]{:S(2)}) collective-permute-start(f16[4,4,2560]{2,1,0:T(4,128)(2,1)S(1)} %get-tuple-element.24), channel_id=1, source_target_pairs={{0,4},{1,5},{2,6},{3,7},{4,0},{5,1},{6,2},{7,3},{8,12},{9,13},{10,... | collective-permute-start | bytes 245768 | tf_op jit(solution)/shard_map/ppermute | solution.py:28
  64.6 5.7 %collective-permute-start.17 = (f16[4,4,2560]{2,1,0:T(4,128)(2,1)S(1)}, f16[4,4,2560]{2,1,0:T(4,128)(2,1)S(1)}, u32[]{:S(2)}, u32[]{:S(2)}) collective-permute-start(f16[4,4,2560]{2,1,0:T(4,128)(2,1)S(1)} %get-tuple-element.23), channel_id=1, source_target_pairs={{0,6},{1,7},{2,0},{3,1},{4,2},{5,3},{6,4},{7,5},{8,14},{9,15},{10,... | collective-permute-start | bytes 245768 | tf_op jit(solution)/shard_map/ppermute | solution.py:28
  70.3 14.3 %copy-start.5 = (f32[1,4,8192]{2,1,0:T(4,128)S(1)}, f32[1,4,8192]{2,1,0:T(4,128)}, u32[]{:S(2)}) copy-start(f32[1,4,8192]{2,1,0:T(4,128)} %param.11) | copy-start | bytes 393220
  70.3 14.3 %copy-start.6 = (f32[1,4,8192]{2,1,0:T(4,128)S(1)}, f32[1,4,8192]{2,1,0:T(4,128)}, u32[]{:S(2)}) copy-start(f32[1,4,8192]{2,1,0:T(4,128)} %param.12) | copy-start | bytes 393220
  70.4 14.3 %copy-start.7 = (f32[1,4,8192]{2,1,0:T(4,128)S(1)}, f32[1,4,8192]{2,1,0:T(4,128)}, u32[]{:S(2)}) copy-start(f32[1,4,8192]{2,1,0:T(4,128)} %param.13) | copy-start | bytes 393220
  70.6 11.3 %collective-permute-start.18 = (f16[4,8192]{1,0:T(4,128)(2,1)S(1)}, f16[4,8192]{1,0:T(4,128)(2,1)S(1)}, u32[]{:S(2)}, u32[]{:S(2)}) collective-permute-start(f16[4,8192]{1,0:T(4,128)(2,1)S(1)} %get-tuple-element.25), channel_id=1, source_target_pairs={{0,16},{1,17},{2,18},{3,19},{4,20},{5,21},{6,22},{7,23},{8,24},{9,... | collective-permute-start | bytes 196616 | tf_op jit(solution)/shard_map/ppermute | solution.py:36
  73.9 8.2 %collective-permute-start.19 = (f16[4,8192]{1,0:T(4,128)(2,1)S(1)}, f16[4,8192]{1,0:T(4,128)(2,1)S(1)}, u32[]{:S(2)}, u32[]{:S(2)}) collective-permute-start(f16[4,8192]{1,0:T(4,128)(2,1)S(1)} %get-tuple-element.27), channel_id=1, source_target_pairs={{0,32},{1,33},{2,34},{3,35},{4,36},{5,37},{6,38},{7,39},{8,40},{9,... | collective-permute-start | bytes 196616 | tf_op jit(solution)/shard_map/ppermute | solution.py:36
  79.0 5.7 %collective-permute-start.20 = (f16[4,8192]{1,0:T(4,128)(2,1)S(1)}, f16[4,8192]{1,0:T(4,128)(2,1)S(1)}, u32[]{:S(2)}, u32[]{:S(2)}) collective-permute-start(f16[4,8192]{1,0:T(4,128)(2,1)S(1)} %get-tuple-element.26), channel_id=1, source_target_pairs={{0,48},{1,49},{2,50},{3,51},{4,52},{5,53},{6,54},{7,55},{8,56},{9,... | collective-permute-start | bytes 196616 | tf_op jit(solution)/shard_map/ppermute | solution.py:36
  81.7 4.0 %copy-start.1 = (f32[32,8192]{1,0:T(8,128)S(1)}, f32[32,8192]{1,0:T(8,128)}, u32[]{:S(2)}) copy-start(f32[32,8192]{1,0:T(8,128)} %param.7) | copy-start | bytes 3145732
  81.7 4.0 %copy-start.3 = (f32[32,8192]{1,0:T(8,128)S(1)}, f32[32,8192]{1,0:T(8,128)}, u32[]{:S(2)}) copy-start(f32[32,8192]{1,0:T(8,128)} %param.9) | copy-start | bytes 3145732
  81.7 3.9 %collective-permute-start.2 = (f32[16,8192]{1,0:T(8,128)S(1)}, f32[16,8192]{1,0:T(8,128)S(1)}, u32[]{:S(2)}, u32[]{:S(2)}) collective-permute-start(f32[16,8192]{1,0:T(8,128)S(1)} %add_multiply_fusion.2), channel_id=1, source_target_pairs={{0,64},{64,0},{128,192},{192,128},{1,65},{65,1},{129,193},{193,129... | collective-permute-start | bytes 1572872 | tf_op jit(solution)/shard_map/ppermute | solution.py:110

commit v2 on v0

v2 whole, which is shorter than its diff:
```python
import jax
import jax.numpy as jnp
from jax import lax
from jax.experimental import pallas as pl
from jax.experimental.pallas import tpu as pltpu
from jax.sharding import PartitionSpec as P

BLOCK = 128
STEP = 8
NZ, NY, NH = 8, 4, 2
F32, F16, BF16 = jnp.float32, jnp.float16, jnp.bfloat16
COLS_Y, COLS_H, COLS_Z = 3072, 2560, 2560
FRAG_SCALE = 2048.0


def place(z, y, h):
    return ((z % NZ) * NY + y % NY) * NH + h % NH


def perm_of(step):
    return [
        (place(z, y, h), place(*step(z, y, h)))
        for z in range(NZ)
        for y in range(NY)
        for h in range(NH)
    ]


def along_y(x, k):
    return lax.ppermute(x, "fsdp", perm_of(lambda z, y, h: (z, y + k, h)))


def along_h(x):
    return lax.ppermute(x, "fsdp", perm_of(lambda z, y, h: (z, y, h + 1)))


def along_z(x, k):
    return lax.ppermute(x, "fsdp", perm_of(lambda z, y, h: (z + k, y, h)))


def pair_z(x, shift):
    return lax.ppermute(
        x, "fsdp", perm_of(lambda z, y, h: ((((z + shift) % NZ) ^ 1) - shift, y, h))
    )


def swap_core(x):
    return lax.ppermute(x, "replica", [(0, 1), (1, 0), (2, 3), (3, 2)])


def take(x, index, axis):
    return lax.dynamic_index_in_dim(x, index, axis, keepdims=False)


def rows_of(x, h, axis):
    low = lax.slice_in_dim(x, 0, 4, axis=axis)
    high = lax.slice_in_dim(x, 4, 8, axis=axis)
    return jnp.where(h == 0, low, high)


def spread(x, me, size, axis):
    others = [take(x, lax.rem(me + k, size), axis).astype(F16) for k in range(1, size)]
    return take(x, me, axis), others


def gather(x, parts, factor):
    for part in parts:
        x = x + part.astype(F32)
    return x * factor


def decode(g, l, mine, theirs):
    core = lax.rem(lax.axis_index("replica"), 2)
    half = g.shape[0] // 2
    for i in range(g.shape[1] // BLOCK):
        at = slice(i * BLOCK, (i + 1) * BLOCK)
        delta = g[:, at] - l[:, at]
        amax = jnp.max(jnp.abs(delta), axis=1, keepdims=True)
        scale = ((amax + 1e-06) / 448.0).astype(BF16).astype(F32)
        decoded = (delta / scale) * scale
        low, high = decoded[:half], decoded[half:]
        mine[:, at] = jnp.where(core == 0, low, high)
        theirs[:, at] = jnp.where(core == 0, high, low)


def deal_kernel(
    g, frag_g, frag_l, a1, a2, a3, a0, c_send, c_own, b_send, b_own, mine_out, theirs_out, *scratch
):
    c_all, c_s, c_o, fg, fl, mine, theirs, a_all, b_all, sems = scratch
    f = lax.axis_index("fsdp")
    y, h, p = lax.rem(f // NH, NY), lax.rem(f, NH), lax.rem(f // (NY * NH), 2)
    first, second = COLS_Y, COLS_Y + COLS_H

    def start(src, dst, i):
        copy = pltpu.make_async_copy(src, dst, sems.at[i])
        copy.start()
        return copy

    fg_in = start(frag_g, fg, 0)
    fl_in = start(frag_l, fl, 1)
    a_in = [start(g.at[:, :, lax.rem(y + k, NY), :, :first], a_all.at[k], 2 + k) for k in range(NY)]
    b_in = [start(g.at[:, q, :, :, second:], b_all.at[i], 6 + i) for i, q in enumerate((1 - p, p))]
    c_in = start(g.at[:, :, :, :, first:second], c_all, 8)
    fg_in.wait()
    fl_in.wait()
    decode(fg, fl, mine, theirs)
    dealt = [start(mine, mine_out, 9), start(theirs, theirs_out, 10)]
    for k, out in enumerate((a0, a1, a2, a3)):
        a_in[k].wait()
        dealt.append(start(a_all.at[k], out, 11 + k))
    for i, out in enumerate((b_send, b_own)):
        b_in[i].wait()
        dealt.append(start(b_all.at[i], out, 15 + i))
    c_in.wait()
    for i in range(NZ // 2):
        for q in range(2):
            for j in range(NY):
                low, high = c_all[i, q, j, 0:4, :], c_all[i, q, j, 4:8, :]
                c_s[i, q, j] = jnp.where(h == 0, high, low)
                c_o[i, q, j] = jnp.where(h == 0, low, high)
    dealt.append(start(c_s, c_send, 17))
    dealt.append(start(c_o, c_own, 18))
    for copy in dealt:
        copy.wait()


def deal(g, frag_g, frag_l):
    rows, width = frag_g.shape
    a = jax.ShapeDtypeStruct((NZ // 2, 2, 8, COLS_Y), BF16)
    b = jax.ShapeDtypeStruct((NZ // 2, NY, 8, COLS_Z), BF16)
    c = jax.ShapeDtypeStruct((NZ // 2, 2, NY, 4, COLS_H), BF16)
    half = jax.ShapeDtypeStruct((rows // 2, width), F32)
    anywhere = pl.BlockSpec(memory_space=pl.ANY)
    hbm = pl.BlockSpec(memory_space=pltpu.HBM)
    return pl.pallas_call(
        deal_kernel,
        out_shape=(a, a, a, a, c, c, b, b, half, half),
        in_specs=[hbm] * 3,
        out_specs=(anywhere,) * 10,
        scratch_shapes=[
            pltpu.VMEM((NZ // 2, 2, NY, 8, COLS_H), BF16),
            pltpu.VMEM((NZ // 2, 2, NY, 4, COLS_H), BF16),
            pltpu.VMEM((NZ // 2, 2, NY, 4, COLS_H), BF16),
            pltpu.VMEM((rows, width), F32),
            pltpu.VMEM((rows, width), F32),
            pltpu.VMEM((rows // 2, width), F32),
            pltpu.VMEM((rows // 2, width), F32),
            pltpu.VMEM((NY, NZ // 2, 2, 8, COLS_Y), BF16),
            pltpu.VMEM((2, NZ // 2, NY, 8, COLS_Z), BF16),
            pltpu.SemaphoreType.DMA((19,)),
        ],
        compiler_params=pltpu.CompilerParams(vmem_limit_bytes=18 << 20),
        cost_estimate=pl.CostEstimate(
            flops=8 * rows * width, bytes_accessed=12 << 20, transcendentals=0
        ),
    )(*(pltpu.with_memory_space_constraint(x, pltpu.HBM) for x in (g, frag_g, frag_l)))


def sums(g, frag, f):
    z, y, h = f // (NY * NH), (f // NH) % NY, f % NH
    p, j = z % 2, z // 2
    a1, a2, a3, a0, c_send, c_own, b_send, b_own, mine, theirs = deal(
        g.reshape(NZ // 2, 2, NY, 8, g.shape[-1]), *frag
    )
    together = lax.optimization_barrier
    a_parts = [along_y(a2, 2), along_y(a1, 1), along_y(a3, 3)]
    c_part = along_h(c_send)
    b_part = pair_z(b_send, 0)
    near = swap_core(theirs)
    pair = ((mine + near) * FRAG_SCALE).astype(F16)
    a0, c_own, b_own, a_parts, c_part, b_part = together(
        (a0, c_own, b_own, a_parts, c_part, b_part)
    )
    a = a0.astype(F32)
    for part in a_parts:
        a = a + part.astype(F32)
    a = a * 16.0
    b = (b_own.astype(F32) + b_part.astype(F32)) * 32.0
    c = (c_own.astype(F32) + c_part.astype(F32)) * 32.0
    a, a_send = rows_of(a, h, 2), rows_of(a, 1 - h, 2).astype(F16)
    b, b_sends = spread(b, y, NY, 1)
    c, c_send = take(c, p, 1), take(c, 1 - p, 1).astype(F16)
    a, a_send, b, b_sends, c, c_send = together((a, a_send, b, b_sends, c, c_send))
    b_parts = [along_y(b_sends[k - 1], k) for k in (2, 1, 3)]
    a_part = along_h(a_send)
    far = lax.ppermute(pair, "replica", [(0, 2), (2, 0), (1, 3), (3, 1)])
    c_part = pair_z(c_send, 0)
    a, a_part, b, b_parts, c, c_part, pair, far = together(
        (a, a_part, b, b_parts, c, c_part, pair, far)
    )
    a = (a + a_part.astype(F32)) * 0.5
    b = gather(b, b_parts, 0.25)
    c = (c + c_part.astype(F32)) * 0.5
    mine = (pair.astype(F32) + far.astype(F32)) * (1.0 / FRAG_SCALE)
    a, a_send = take(a, p, 1), take(a, 1 - p, 1).astype(F16)
    b, b_send = rows_of(b, h, 1), rows_of(b, 1 - h, 1).astype(F16)
    c, c_sends = spread(c, y, NY, 1)
    a, a_send, b, b_send, c, c_sends, mine = together(
        (a, a_send, b, b_send, c, c_sends, mine)
    )
    theirs = swap_core(mine)
    c_parts = [along_y(c_sends[k - 1], k) for k in (2, 1, 3)]
    b_part = along_h(b_send)
    a_part = pair_z(a_send, 0)
    a, a_part, b, b_part, c, c_parts, mine, theirs = together(
        (a, a_part, b, b_part, c, c_parts, mine, theirs)
    )
    a = (a + a_part.astype(F32)) * 0.5
    b = (b + b_part.astype(F32)) * 0.5
    c = gather(c, c_parts, 0.25)
    t, t_sends = spread(jnp.concatenate([a, c, b], axis=-1), j, NZ // 2, 0)
    t, t_sends = together((t, t_sends))
    t_parts = [along_z(x, 2 * (k + 1)) for k, x in enumerate(t_sends)]
    core = lax.rem(lax.axis_index("replica"), 2)
    low, high = jnp.where(core == 0, mine, theirs), jnp.where(core == 0, theirs, mine)
    return gather(t, t_parts, 0.25), jnp.concatenate([low, high], axis=0)


def on_device(global_frag, local_frag, outer_mom, grads, inner_param, inner_m, inner_v):
    f = lax.axis_index("fsdp")
    groups = lax.axis_size("fsdp")
    summed, total = sums(grads[0, 0], (global_frag, local_frag[0]), f)
    average = 0.25 * total
    new_mom = 0.9 * outer_mom + average
    new_global = global_frag - 0.7 * (average + 0.9 * new_mom)
    gmean = (summed / groups)[None]
    new_m = 0.9 * inner_m + 0.1 * gmean
    new_v = 0.95 * inner_v + 0.05 * gmean * gmean
    m_hat = new_m / (1.0 - 0.9**STEP)
    v_hat = new_v / (1.0 - 0.95**STEP)
    new_param = inner_param - 0.0003 * (m_hat / (jnp.sqrt(v_hat) + 1e-08) + 0.1 * inner_param)
    return (new_global, new_mom, new_param, new_m, new_v)


def solution(mesh):
    placed = (
        P("fsdp", None),
        P("replica", "fsdp", None),
        P("fsdp", None),
        P("replica", "fsdp", None, None),
        P("replica", "fsdp", None),
        P("replica", "fsdp", None),
        P("replica", "fsdp", None),
    )
    return jax.shard_map(
        on_device,
        mesh=mesh,
        in_specs=placed,
        out_specs=(
            P("fsdp", None),
            P("fsdp", None),
            P("replica", "fsdp", None),
            P("replica", "fsdp", None),
            P("replica", "fsdp", None),
        ),
        check_vma=False,
    )
```

time: 803 us -> 74.2 us (0.09)
  waiting for transfers between devices: 766 us -> 27.2 us
  starting transfers between devices: 0.08 us -> 33.6 us
  between operations: 14.9 us -> 0.85 us
    unnamed x3 -> x0, waiting for transfers between devices: 724 us -> none
    psum x1 -> x0, waiting for transfers between devices: 41.9 us -> none  [on_device(): total = lax.psum(decoded, 'replica')]
    ppermute x0 -> x21, starting transfers between devices: none -> 33.6 us  [the longest x3 10.5 us: along_z(): return lax.ppermute(x, 'fsdp', perm_of(lambda z, y, h: (z + k, y, h)))]
    ppermute x0 -> x21, waiting for transfers between devices: none -> 27.2 us  [the longest x9 22 us: along_y(): return lax.ppermute(x, 'fsdp', perm_of(lambda z, y, h: (z, y + k, h)))]
  transfers between devices with their start and end apart: 2 -> 21, of which waited for: 2 -> 13; matrix products, arithmetic and copies ran while one was open for 1% -> 9% of each run, Pallas kernels for 0% -> 0%
where the time goes in v2:
time: 74.2 us; the launch traced here: 74 us
  starting transfers between devices  33.6 us (45%)
  waiting for transfers between devices  27.2 us (37%)
  other arithmetic  8.45 us (11%)
  Pallas kernels  3.79 us (5%)
  between operations  0.85 us (1%)
    ppermute x9, waiting for transfers between devices, along_y(): return lax.ppermute(x, 'fsdp', perm_of(lambda z, y, h: (z, y + k, h)))  22 us
    ppermute x3, starting transfers between devices, along_z(): return lax.ppermute(x, 'fsdp', perm_of(lambda z, y, h: (z + k, y, h)))  10.5 us
    ppermute x9, starting transfers between devices, along_y(): return lax.ppermute(x, 'fsdp', perm_of(lambda z, y, h: (z, y + k, h)))  10.1 us
    ppermute x3, starting transfers between devices, along_h(): return lax.ppermute(x, 'fsdp', perm_of(lambda z, y, h: (z, y, h + 1)))  6.61 us
    ppermute x3, starting transfers between devices, pair_z(): lax.ppermute(x, 'fsdp', perm_of(lambda z, y, h: (((z + shift) % NZ ^ 1) -...  4.72 us
    pallas_call x1, Pallas kernels, deal(): pl.pallas_call(deal_kernel, out_shape=(a, a, a, a, c, c, b, b, half, half...  3.79 us
    ppermute x3, waiting for transfers between devices, along_h(): return lax.ppermute(x, 'fsdp', perm_of(lambda z, y, h: (z, y, h + 1)))  3.34 us
    ppermute x3, waiting for transfers between devices, along_z(): return lax.ppermute(x, 'fsdp', perm_of(lambda z, y, h: (z + k, y, h)))  1.7 us
  transfers between devices with their start and end apart: 21, of which 13 were waited for; matrix products, arithmetic and copies ran while one was open for 9% of the time, Pallas kernels for 0%

profile of v2, /device:TPU:24, one launch (start us, length us, event | category | flops | bytes accessed | tf_op | source)
XLA Modules:
  0.0 74.0 jit_solution(2428323953173479409)
XLA Ops:
  0.6 3.8 %shard_map.110 = (bf16[4,2,8,3072]{3,2,1,0:T(8,128)(2,1)}, bf16[4,2,8,3072]{3,2,1,0:T(8,128)(2,1)}, bf16[4,2,8,3072]{3,2,1,0:T(8,128)(2,1)}, bf16[4,2,8,3072]{3,...) custom-call(bf16[4,2,4,8,8192]{4,3,2,1,0:T(8,128)(2,1)} %bitcast.56,, ...), custom_call_target="tpu_custom_call" | custom-call | flops 2097152 | bytes 12582912 | tf_op jit(solution)/shard_map/pallas_call | solution.py:135
  4.4 0.1 collective-permute-start.10
  4.5 1.3 %collective-permute-start = (bf16[4,2,8,3072]{3,2,1,0:T(8,128)(2,1)}, bf16[4,2,8,3072]{3,2,1,0:T(8,128)(2,1)}, u32[]{:S(2)}, u32[]{:S(2)}) collective-permute-start(bf16[4,2,8,3072]{3,2,1,0:T(8,128)(2,1)} %get-tuple-element.67), channel_id=1, source_target_pairs={{0,4},{1,5},{2,6},{3,7},{4,0},{5,1},{6,2},{7,3},{8,12},{9,13},{10,... | collective-permute-start | bytes 1179656 | tf_op jit(solution)/shard_map/ppermute | solution.py:30
  5.9 2.2 %collective-permute-start.1 = (bf16[4,2,8,3072]{3,2,1,0:T(8,128)(2,1)}, bf16[4,2,8,3072]{3,2,1,0:T(8,128)(2,1)}, u32[]{:S(2)}, u32[]{:S(2)}) collective-permute-start(bf16[4,2,8,3072]{3,2,1,0:T(8,128)(2,1)} %get-tuple-element.68), channel_id=1, source_target_pairs={{0,2},{1,3},{2,4},{3,5},{4,6},{5,7},{6,0},{7,1},{8,10},{9,11},{10,... | collective-permute-start | bytes 1179656 | tf_op jit(solution)/shard_map/ppermute | solution.py:30
  8.0 3.0 %collective-permute-start.3 = (bf16[4,2,4,4,2560]{4,3,2,1,0:T(4,128)(2,1)S(1)}, bf16[4,2,4,4,2560]{4,3,2,1,0:T(4,128)(2,1)}, u32[]{:S(2)}, u32[]{:S(2)}) collective-permute-start(bf16[4,2,4,4,2560]{4,3,2,1,0:T(4,128)(2,1)S(1)} %get-tuple-element.70), channel_id=1, source_target_pairs={{0,1},{1,0},{2,3},{3,2},{4,5},{5,4},{6,7},{7,6},{8,9},{9,8},{10,11... | collective-permute-start | bytes 1966088 | tf_op jit(solution)/shard_map/ppermute | solution.py:34
  11.1 1.9 %collective-permute-start.4 = (bf16[4,4,8,2560]{3,2,1,0:T(8,128)(2,1)S(1)}, bf16[4,4,8,2560]{3,2,1,0:T(8,128)(2,1)S(1)}, u32[]{:S(2)}, u32[]{:S(2)}) collective-permute-start(bf16[4,4,8,2560]{3,2,1,0:T(8,128)(2,1)S(1)} %get-tuple-element.71), channel_id=1, source_target_pairs={{0,8},{1,9},{2,10},{3,11},{4,12},{5,13},{6,14},{7,15},{8,0},{9,1},... | collective-permute-start | bytes 1966088 | tf_op jit(solution)/shard_map/ppermute | solution.py:42
  13.0 1.1 %multiply_convert_fusion = f16[16,8192]{1,0:T(8,128)(2,1)S(1)} fusion(f32[16,8192]{1,0:T(8,128)S(1)} %get-tuple-element.88, f32[16,8192]{1,0:T(8,128)} %collective-permute-done.10), kind=kLoop, calls=%fused_computation.11 | loop fusion | flops 393216 | bytes 1310720 | tf_op jit(solution)/shard_map/convert_element_type | solution.py:170
  14.1 4.3 %collective-permute-done = bf16[4,2,8,3072]{3,2,1,0:T(8,128)(2,1)} collective-permute-done((bf16[4,2,8,3072]{3,2,1,0:T(8,128)(2,1)}, bf16[4,2,8,3072]{3,2,1,0:T(8,128)(2,1)}, u32[]{:S(2)}, u32[]{:S(2)}) %collective-permute-start) | collective-permute-done | bytes 393248 | tf_op jit(solution)/shard_map/ppermute | solution.py:30
  18.4 1.5 %collective-permute-start.11 = (f16[16,8192]{1,0:T(8,128)(2,1)S(1)}, f16[16,8192]{1,0:T(8,128)(2,1)S(1)}, u32[]{:S(2)}, u32[]{:S(2)}) collective-permute-start(f16[16,8192]{1,0:T(8,128)(2,1)S(1)} %multiply_convert_fusion), channel_id=1, source_target_pairs={{0,128},{128,0},{64,192},{192,64},{1,129},{129,1},{65,193},{193,65... | collective-permute-start | bytes 786440 | tf_op jit(solution)/shard_map/ppermute | solution.py:186
  19.9 5.7 %collective-permute-done.1 = bf16[4,2,8,3072]{3,2,1,0:T(8,128)(2,1)} collective-permute-done((bf16[4,2,8,3072]{3,2,1,0:T(8,128)(2,1)}, bf16[4,2,8,3072]{3,2,1,0:T(8,128)(2,1)}, u32[]{:S(2)}, u32[]{:S(2)}) %collective-permute-start.1) | collective-permute-done | bytes 393248 | tf_op jit(solution)/shard_map/ppermute | solution.py:30
  25.6 0.7 collective-permute-done.2
  26.3 0.9 %collective-permute-done.3 = bf16[4,2,4,4,2560]{4,3,2,1,0:T(4,128)(2,1)} collective-permute-done((bf16[4,2,4,4,2560]{4,3,2,1,0:T(4,128)(2,1)S(1)}, bf16[4,2,4,4,2560]{4,3,2,1,0:T(4,128)(2,1)}, u32[]{:S(2)}, u32[]{:S(2)}) %collective-permute-start.3) | collective-permute-done | bytes 655392 | tf_op jit(solution)/shard_map/ppermute | solution.py:34
  27.3 0.2 collective-permute-done.4
  27.5 0.2 add_multiply_fusion.1
  27.7 1.5 %add_multiply_fusion = f32[4,2,4,4,2560]{4,3,2,1,0:T(4,128)S(1)} fusion(bf16[4,2,4,4,2560]{4,3,2,1,0:T(4,128)(2,1)} %collective-permute-done.3, bf16[4,2,4,4,2560]{4,3,2,1,0:T(4,128)(2,1)S(1)} %get-tuple-element.78), kind=kLoop, calls=%fused_computation | loop fusion | flops 1310720 | bytes 2621440 | tf_op jit(solution)/shard_map/mul | solution.py:179
  29.2 1.4 %add_multiply_fusion.2 = f32[4,2,8,3072]{3,2,1,0:T(8,128)S(1)} fusion(bf16[4,2,8,3072]{3,2,1,0:T(8,128)(2,1)} %collective-permute-done.2, bf16[4,2,8,3072]{3,2,1,0:T(8,128)(2,1)} %collective-permute-done.1, bf16[4,2,8,3072]{3,2,1,0:T(8,128)(2,1)} %collective-permute-done, bf16[4,2,8,3072]{3,2,1,0:T(8,128)(2,1)S(1)} %get-tuple-element.72), kind=kLoop, calls=%fused_computation.5 | loop fusion | flops 1572864 | bytes 2359296 | tf_op jit(solution)/shard_map/mul | solution.py:177
  30.7 0.2 select_convert_fusion
  30.8 0.2 fusion
  31.0 0.1 fusion.1
  31.1 1.8 %collective-permute-start.9 = (f16[4,4,4,2560]{3,2,1,0:T(4,128)(2,1)S(1)}, f16[4,4,4,2560]{3,2,1,0:T(4,128)(2,1)S(1)}, u32[]{:S(2)}, u32[]{:S(2)}) collective-permute-start(f16[4,4,4,2560]{3,2,1,0:T(4,128)(2,1)S(1)} %get-tuple-element.87), channel_id=1, source_target_pairs={{0,8},{1,9},{2,10},{3,11},{4,12},{5,13},{6,14},{7,15},{8,0},{9,1},... | collective-permute-start | bytes 983048 | tf_op jit(solution)/shard_map/ppermute | solution.py:42
  32.9 3.0 %collective-permute-start.5 = (f16[4,2,4,3072]{3,2,1,0:T(4,128)(2,1)S(1)}, f16[4,2,4,3072]{3,2,1,0:T(4,128)(2,1)S(1)}, u32[]{:S(2)}, u32[]{:S(2)}) collective-permute-start(f16[4,2,4,3072]{3,2,1,0:T(4,128)(2,1)S(1)} %get-tuple-element.81), channel_id=1, source_target_pairs={{0,1},{1,0},{2,3},{3,2},{4,5},{5,4},{6,7},{7,6},{8,9},{9,8},{10,11... | collective-permute-start | bytes 589832 | tf_op jit(solution)/shard_map/ppermute | solution.py:34
  35.9 2.2 %collective-permute-start.6 = (f16[4,8,2560]{2,1,0:T(8,128)(2,1)S(1)}, f16[4,8,2560]{2,1,0:T(8,128)(2,1)S(1)}, u32[]{:S(2)}, u32[]{:S(2)}) collective-permute-start(f16[4,8,2560]{2,1,0:T(8,128)(2,1)S(1)} %get-tuple-element.83), channel_id=1, source_target_pairs={{0,4},{1,5},{2,6},{3,7},{4,0},{5,1},{6,2},{7,3},{8,12},{9,13},{10,... | collective-permute-start | bytes 491528 | tf_op jit(solution)/shard_map/ppermute | solution.py:30
  38.1 1.1 %collective-permute-start.7 = (f16[4,8,2560]{2,1,0:T(8,128)(2,1)S(1)}, f16[4,8,2560]{2,1,0:T(8,128)(2,1)S(1)}, u32[]{:S(2)}, u32[]{:S(2)}) collective-permute-start(f16[4,8,2560]{2,1,0:T(8,128)(2,1)S(1)} %get-tuple-element.84), channel_id=1, source_target_pairs={{0,2},{1,3},{2,4},{3,5},{4,6},{5,7},{6,0},{7,1},{8,10},{9,11},{10,... | collective-permute-start | bytes 491528 | tf_op jit(solution)/shard_map/ppermute | solution.py:30
  39.2 0.9 %collective-permute-start.8 = (f16[4,8,2560]{2,1,0:T(8,128)(2,1)S(1)}, f16[4,8,2560]{2,1,0:T(8,128)(2,1)S(1)}, u32[]{:S(2)}, u32[]{:S(2)}) collective-permute-start(f16[4,8,2560]{2,1,0:T(8,128)(2,1)S(1)} %get-tuple-element.85), channel_id=1, source_target_pairs={{0,6},{1,7},{2,0},{3,1},{4,2},{5,3},{6,4},{7,5},{8,14},{9,15},{10,... | collective-permute-start | bytes 491528 | tf_op jit(solution)/shard_map/ppermute | solution.py:30
  40.1 3.7 %collective-permute-done.6 = f16[4,8,2560]{2,1,0:T(8,128)(2,1)S(1)} collective-permute-done((f16[4,8,2560]{2,1,0:T(8,128)(2,1)S(1)}, f16[4,8,2560]{2,1,0:T(8,128)(2,1)S(1)}, u32[]{:S(2)}, u32[]{:S(2)}) %collective-permute-start.6) | collective-permute-done | bytes 163872 | tf_op jit(solution)/shard_map/ppermute | solution.py:30
  43.8 1.3 %collective-permute-done.7 = f16[4,8,2560]{2,1,0:T(8,128)(2,1)S(1)} collective-permute-done((f16[4,8,2560]{2,1,0:T(8,128)(2,1)S(1)}, f16[4,8,2560]{2,1,0:T(8,128)(2,1)S(1)}, u32[]{:S(2)}, u32[]{:S(2)}) %collective-permute-start.7) | collective-permute-done | bytes 163872 | tf_op jit(solution)/shard_map/ppermute | solution.py:30
  45.1 0.6 collective-permute-done.8
  45.7 0.1 add_multiply_fusion.5
  46.1 0.2 add_multiply_fusion.3
  46.3 0.1 fusion.5
  46.5 0.1 collective-permute-start.17
  46.6 0.6 collective-permute-start.13
  47.2 1.0 %collective-permute-start.12 = (f16[4,4,3072]{2,1,0:T(4,128)(2,1)S(1)}, f16[4,4,3072]{2,1,0:T(4,128)(2,1)S(1)}, u32[]{:S(2)}, u32[]{:S(2)}) collective-permute-start(f16[4,4,3072]{2,1,0:T(4,128)(2,1)S(1)} %get-tuple-element.101), channel_id=1, source_target_pairs={{0,8},{1,9},{2,10},{3,11},{4,12},{5,13},{6,14},{7,15},{8,0},{9,1},... | collective-permute-start | bytes 294920 | tf_op jit(solution)/shard_map/ppermute | solution.py:42
  48.2 0.9 %collective-permute-start.14 = (f16[4,4,2560]{2,1,0:T(4,128)(2,1)S(1)}, f16[4,4,2560]{2,1,0:T(4,128)(2,1)S(1)}, u32[]{:S(2)}, u32[]{:S(2)}) collective-permute-start(f16[4,4,2560]{2,1,0:T(4,128)(2,1)S(1)} %get-tuple-element.105), channel_id=1, source_target_pairs={{0,4},{1,5},{2,6},{3,7},{4,0},{5,1},{6,2},{7,3},{8,12},{9,13},{10,... | collective-permute-start | bytes 245768 | tf_op jit(solution)/shard_map/ppermute | solution.py:30
  49.0 1.6 %collective-permute-start.15 = (f16[4,4,2560]{2,1,0:T(4,128)(2,1)S(1)}, f16[4,4,2560]{2,1,0:T(4,128)(2,1)S(1)}, u32[]{:S(2)}, u32[]{:S(2)}) collective-permute-start(f16[4,4,2560]{2,1,0:T(4,128)(2,1)S(1)} %get-tuple-element.106), channel_id=1, source_target_pairs={{0,2},{1,3},{2,4},{3,5},{4,6},{5,7},{6,0},{7,1},{8,10},{9,11},{10,... | collective-permute-start | bytes 245768 | tf_op jit(solution)/shard_map/ppermute | solution.py:30
  50.6 2.4 %collective-permute-done.13 = f16[4,4,2560]{2,1,0:T(4,128)(2,1)S(1)} collective-permute-done((f16[4,4,2560]{2,1,0:T(4,128)(2,1)S(1)}, f16[4,4,2560]{2,1,0:T(4,128)(2,1)S(1)}, u32[]{:S(2)}, u32[]{:S(2)}) %collective-permute-start.13) | collective-permute-done | bytes 81952 | tf_op jit(solution)/shard_map/ppermute | solution.py:34
  53.0 1.1 %collective-permute-done.14 = f16[4,4,2560]{2,1,0:T(4,128)(2,1)S(1)} collective-permute-done((f16[4,4,2560]{2,1,0:T(4,128)(2,1)S(1)}, f16[4,4,2560]{2,1,0:T(4,128)(2,1)S(1)}, u32[]{:S(2)}, u32[]{:S(2)}) %collective-permute-start.14) | collective-permute-done | bytes 81952 | tf_op jit(solution)/shard_map/ppermute | solution.py:30
  54.1 0.6 collective-permute-done.15
  54.7 3.9 %collective-permute-done.16 = f16[4,4,2560]{2,1,0:T(4,128)(2,1)S(1)} collective-permute-done((f16[4,4,2560]{2,1,0:T(4,128)(2,1)S(1)}, f16[4,4,2560]{2,1,0:T(4,128)(2,1)S(1)}, u32[]{:S(2)}, u32[]{:S(2)}) %collective-permute-start.16) | collective-permute-done | bytes 81952 | tf_op jit(solution)/shard_map/ppermute | solution.py:30
  58.7 0.1 add_multiply_fusion.8
  58.8 0.1 pad_maximum_fusion
  59.0 0.1 fusion.10
  59.1 3.3 %collective-permute-start.18 = (f16[4,8192]{1,0:T(4,128)(2,1)S(1)}, f16[4,8192]{1,0:T(4,128)(2,1)S(1)}, u32[]{:S(2)}, u32[]{:S(2)}) collective-permute-start(f16[4,8192]{1,0:T(4,128)(2,1)S(1)} %get-tuple-element.120), channel_id=1, source_target_pairs={{0,16},{1,17},{2,18},{3,19},{4,20},{5,21},{6,22},{7,23},{8,24},{9,... | collective-permute-start | bytes 196616 | tf_op jit(solution)/shard_map/ppermute | solution.py:38
  62.4 4.5 %collective-permute-start.19 = (f16[4,8192]{1,0:T(4,128)(2,1)S(1)}, f16[4,8192]{1,0:T(4,128)(2,1)S(1)}, u32[]{:S(2)}, u32[]{:S(2)}) collective-permute-start(f16[4,8192]{1,0:T(4,128)(2,1)S(1)} %get-tuple-element.121), channel_id=1, source_target_pairs={{0,32},{1,33},{2,34},{3,35},{4,36},{5,37},{6,38},{7,39},{8,40},{9,... | collective-permute-start | bytes 196616 | tf_op jit(solution)/shard_map/ppermute | solution.py:38
  66.9 2.7 %collective-permute-start.20 = (f16[4,8192]{1,0:T(4,128)(2,1)S(1)}, f16[4,8192]{1,0:T(4,128)(2,1)S(1)}, u32[]{:S(2)}, u32[]{:S(2)}) collective-permute-start(f16[4,8192]{1,0:T(4,128)(2,1)S(1)} %get-tuple-element.122), channel_id=1, source_target_pairs={{0,48},{1,49},{2,50},{3,51},{4,52},{5,53},{6,54},{7,55},{8,56},{9,... | collective-permute-start | bytes 196616 | tf_op jit(solution)/shard_map/ppermute | solution.py:38
  69.7 1.6 %multiply_subtract_fusion = (f32[32,8192]{1,0:T(8,128)}, f32[32,8192]{1,0:T(8,128)}) fusion(f32[32,8192]{1,0:T(8,128)S(1)} %copy-done, f32[16,8192]{1,0:T(8,128)S(1)} %get-tuple-element.135, f32[16,8192]{1,0:T(8,128)S(1)} %get-tuple-element.134, f32[32,8192]{1,0:T(8,128)S(1)} %copy-done.1), kind=kLoop, calls=%fused_computation.3 | loop fusion | flops 2097152 | bytes 5242880 | tf_op jit(solution)/shard_map/sub | solution.py:225
  71.3 1.7 %collective-permute-done.20 = f16[4,8192]{1,0:T(4,128)(2,1)S(1)} collective-permute-done((f16[4,8192]{1,0:T(4,128)(2,1)S(1)}, f16[4,8192]{1,0:T(4,128)(2,1)S(1)}, u32[]{:S(2)}, u32[]{:S(2)}) %collective-permute-start.20) | collective-permute-done | bytes 65568 | tf_op jit(solution)/shard_map/ppermute | solution.py:38
  73.0 1.0 %multiply_subtract_fusion.1 = (f32[1,4,8192]{2,1,0:T(4,128)}, f32[1,4,8192]{2,1,0:T(4,128)}, f32[1,4,8192]{2,1,0:T(4,128)}) fusion(f32[1,4,8192]{2,1,0:T(4,128)S(1)} %copy-done.2, f16[4,8192]{1,0:T(4,128)(2,1)S(1)} %collective-permute-done.20, f16[4,8192]{1,0:T(4,128)(2,1)S(1)} %collective-permute-done.19, f32[4,8192]{1,0:T(4,128)S(1)} %get-tuple-element.119, ...), kind=kLoop, calls=%fused_computation.39 | loop fusion | flops 720896 | bytes 1114112 | tf_op jit(solution)/shard_map/sub | solution.py:231
  (26 shorter events, 0.5 us)
Async XLA Ops:
  4.4 6.6 %collective-permute-start.10 = (f32[16,8192]{1,0:T(8,128)}, f32[16,8192]{1,0:T(8,128)}, u32[]{:S(2)}, u32[]{:S(2)}) collective-permute-start(f32[16,8192]{1,0:T(8,128)} %get-tuple-element.89), channel_id=1, source_target_pairs={{0,64},{64,0},{128,192},{192,128},{1,65},{65,1},{129,193},{193,129... | collective-permute-start | bytes 1572872 | tf_op jit(solution)/shard_map/ppermute | solution.py:48
  4.5 13.9 %collective-permute-start = (bf16[4,2,8,3072]{3,2,1,0:T(8,128)(2,1)}, bf16[4,2,8,3072]{3,2,1,0:T(8,128)(2,1)}, u32[]{:S(2)}, u32[]{:S(2)}) collective-permute-start(bf16[4,2,8,3072]{3,2,1,0:T(8,128)(2,1)} %get-tuple-element.67), channel_id=1, source_target_pairs={{0,4},{1,5},{2,6},{3,7},{4,0},{5,1},{6,2},{7,3},{8,12},{9,13},{10,... | collective-permute-start | bytes 1179656 | tf_op jit(solution)/shard_map/ppermute | solution.py:30
  5.9 19.8 %collective-permute-start.1 = (bf16[4,2,8,3072]{3,2,1,0:T(8,128)(2,1)}, bf16[4,2,8,3072]{3,2,1,0:T(8,128)(2,1)}, u32[]{:S(2)}, u32[]{:S(2)}) collective-permute-start(bf16[4,2,8,3072]{3,2,1,0:T(8,128)(2,1)} %get-tuple-element.68), channel_id=1, source_target_pairs={{0,2},{1,3},{2,4},{3,5},{4,6},{5,7},{6,0},{7,1},{8,10},{9,11},{10,... | collective-permute-start | bytes 1179656 | tf_op jit(solution)/shard_map/ppermute | solution.py:30
  8.0 18.3 %collective-permute-start.2 = (bf16[4,2,8,3072]{3,2,1,0:T(8,128)(2,1)}, bf16[4,2,8,3072]{3,2,1,0:T(8,128)(2,1)}, u32[]{:S(2)}, u32[]{:S(2)}) collective-permute-start(bf16[4,2,8,3072]{3,2,1,0:T(8,128)(2,1)} %get-tuple-element.69), channel_id=1, source_target_pairs={{0,6},{1,7},{2,0},{3,1},{4,2},{5,3},{6,4},{7,5},{8,14},{9,15},{10,... | collective-permute-start | bytes 1179656 | tf_op jit(solution)/shard_map/ppermute | solution.py:30
  8.0 19.2 %collective-permute-start.3 = (bf16[4,2,4,4,2560]{4,3,2,1,0:T(4,128)(2,1)S(1)}, bf16[4,2,4,4,2560]{4,3,2,1,0:T(4,128)(2,1)}, u32[]{:S(2)}, u32[]{:S(2)}) collective-permute-start(bf16[4,2,4,4,2560]{4,3,2,1,0:T(4,128)(2,1)S(1)} %get-tuple-element.70), channel_id=1, source_target_pairs={{0,1},{1,0},{2,3},{3,2},{4,5},{5,4},{6,7},{7,6},{8,9},{9,8},{10,11... | collective-permute-start | bytes 1966088 | tf_op jit(solution)/shard_map/ppermute | solution.py:34
  11.1 16.4 %collective-permute-start.4 = (bf16[4,4,8,2560]{3,2,1,0:T(8,128)(2,1)S(1)}, bf16[4,4,8,2560]{3,2,1,0:T(8,128)(2,1)S(1)}, u32[]{:S(2)}, u32[]{:S(2)}) collective-permute-start(bf16[4,4,8,2560]{3,2,1,0:T(8,128)(2,1)S(1)} %get-tuple-element.71), channel_id=1, source_target_pairs={{0,8},{1,9},{2,10},{3,11},{4,12},{5,13},{6,14},{7,15},{8,0},{9,1},... | collective-permute-start | bytes 1966088 | tf_op jit(solution)/shard_map/ppermute | solution.py:42
  18.4 20.8 %collective-permute-start.11 = (f16[16,8192]{1,0:T(8,128)(2,1)S(1)}, f16[16,8192]{1,0:T(8,128)(2,1)S(1)}, u32[]{:S(2)}, u32[]{:S(2)}) collective-permute-start(f16[16,8192]{1,0:T(8,128)(2,1)S(1)} %multiply_convert_fusion), channel_id=1, source_target_pairs={{0,128},{128,0},{64,192},{192,64},{1,129},{129,1},{65,193},{193,65... | collective-permute-start | bytes 786440 | tf_op jit(solution)/shard_map/ppermute | solution.py:186
  31.1 14.6 %collective-permute-start.9 = (f16[4,4,4,2560]{3,2,1,0:T(4,128)(2,1)S(1)}, f16[4,4,4,2560]{3,2,1,0:T(4,128)(2,1)S(1)}, u32[]{:S(2)}, u32[]{:S(2)}) collective-permute-start(f16[4,4,4,2560]{3,2,1,0:T(4,128)(2,1)S(1)} %get-tuple-element.87), channel_id=1, source_target_pairs={{0,8},{1,9},{2,10},{3,11},{4,12},{5,13},{6,14},{7,15},{8,0},{9,1},... | collective-permute-start | bytes 983048 | tf_op jit(solution)/shard_map/ppermute | solution.py:42
  32.9 12.8 %collective-permute-start.5 = (f16[4,2,4,3072]{3,2,1,0:T(4,128)(2,1)S(1)}, f16[4,2,4,3072]{3,2,1,0:T(4,128)(2,1)S(1)}, u32[]{:S(2)}, u32[]{:S(2)}) collective-permute-start(f16[4,2,4,3072]{3,2,1,0:T(4,128)(2,1)S(1)} %get-tuple-element.81), channel_id=1, source_target_pairs={{0,1},{1,0},{2,3},{3,2},{4,5},{5,4},{6,7},{7,6},{8,9},{9,8},{10,11... | collective-permute-start | bytes 589832 | tf_op jit(solution)/shard_map/ppermute | solution.py:34
  35.9 7.9 %collective-permute-start.6 = (f16[4,8,2560]{2,1,0:T(8,128)(2,1)S(1)}, f16[4,8,2560]{2,1,0:T(8,128)(2,1)S(1)}, u32[]{:S(2)}, u32[]{:S(2)}) collective-permute-start(f16[4,8,2560]{2,1,0:T(8,128)(2,1)S(1)} %get-tuple-element.83), channel_id=1, source_target_pairs={{0,4},{1,5},{2,6},{3,7},{4,0},{5,1},{6,2},{7,3},{8,12},{9,13},{10,... | collective-permute-start | bytes 491528 | tf_op jit(solution)/shard_map/ppermute | solution.py:30
  38.1 7.0 %collective-permute-start.7 = (f16[4,8,2560]{2,1,0:T(8,128)(2,1)S(1)}, f16[4,8,2560]{2,1,0:T(8,128)(2,1)S(1)}, u32[]{:S(2)}, u32[]{:S(2)}) collective-permute-start(f16[4,8,2560]{2,1,0:T(8,128)(2,1)S(1)} %get-tuple-element.84), channel_id=1, source_target_pairs={{0,2},{1,3},{2,4},{3,5},{4,6},{5,7},{6,0},{7,1},{8,10},{9,11},{10,... | collective-permute-start | bytes 491528 | tf_op jit(solution)/shard_map/ppermute | solution.py:30
  39.2 6.5 %collective-permute-start.8 = (f16[4,8,2560]{2,1,0:T(8,128)(2,1)S(1)}, f16[4,8,2560]{2,1,0:T(8,128)(2,1)S(1)}, u32[]{:S(2)}, u32[]{:S(2)}) collective-permute-start(f16[4,8,2560]{2,1,0:T(8,128)(2,1)S(1)} %get-tuple-element.85), channel_id=1, source_target_pairs={{0,6},{1,7},{2,0},{3,1},{4,2},{5,3},{6,4},{7,5},{8,14},{9,15},{10,... | collective-permute-start | bytes 491528 | tf_op jit(solution)/shard_map/ppermute | solution.py:30
  46.5 12.1 %collective-permute-start.17 = (f32[16,8192]{1,0:T(8,128)S(1)}, f32[16,8192]{1,0:T(8,128)S(1)}, u32[]{:S(2)}, u32[]{:S(2)}) collective-permute-start(f32[16,8192]{1,0:T(8,128)S(1)} %add_multiply_fusion.4), channel_id=1, source_target_pairs={{0,64},{64,0},{128,192},{192,128},{1,65},{65,1},{129,193},{193,129... | collective-permute-start | bytes 1572872 | tf_op jit(solution)/shard_map/ppermute | solution.py:48
  46.6 6.4 %collective-permute-start.13 = (f16[4,4,2560]{2,1,0:T(4,128)(2,1)S(1)}, f16[4,4,2560]{2,1,0:T(4,128)(2,1)S(1)}, u32[]{:S(2)}, u32[]{:S(2)}) collective-permute-start(f16[4,4,2560]{2,1,0:T(4,128)(2,1)S(1)} %get-tuple-element.103), channel_id=1, source_target_pairs={{0,1},{1,0},{2,3},{3,2},{4,5},{5,4},{6,7},{7,6},{8,9},{9,8},{10,11... | collective-permute-start | bytes 245768 | tf_op jit(solution)/shard_map/ppermute | solution.py:34
  47.2 11.4 %collective-permute-start.12 = (f16[4,4,3072]{2,1,0:T(4,128)(2,1)S(1)}, f16[4,4,3072]{2,1,0:T(4,128)(2,1)S(1)}, u32[]{:S(2)}, u32[]{:S(2)}) collective-permute-start(f16[4,4,3072]{2,1,0:T(4,128)(2,1)S(1)} %get-tuple-element.101), channel_id=1, source_target_pairs={{0,8},{1,9},{2,10},{3,11},{4,12},{5,13},{6,14},{7,15},{8,0},{9,1},... | collective-permute-start | bytes 294920 | tf_op jit(solution)/shard_map/ppermute | solution.py:42
  48.2 5.9 %collective-permute-start.14 = (f16[4,4,2560]{2,1,0:T(4,128)(2,1)S(1)}, f16[4,4,2560]{2,1,0:T(4,128)(2,1)S(1)}, u32[]{:S(2)}, u32[]{:S(2)}) collective-permute-start(f16[4,4,2560]{2,1,0:T(4,128)(2,1)S(1)} %get-tuple-element.105), channel_id=1, source_target_pairs={{0,4},{1,5},{2,6},{3,7},{4,0},{5,1},{6,2},{7,3},{8,12},{9,13},{10,... | collective-permute-start | bytes 245768 | tf_op jit(solution)/shard_map/ppermute | solution.py:30
  49.0 5.7 %collective-permute-start.15 = (f16[4,4,2560]{2,1,0:T(4,128)(2,1)S(1)}, f16[4,4,2560]{2,1,0:T(4,128)(2,1)S(1)}, u32[]{:S(2)}, u32[]{:S(2)}) collective-permute-start(f16[4,4,2560]{2,1,0:T(4,128)(2,1)S(1)} %get-tuple-element.106), channel_id=1, source_target_pairs={{0,2},{1,3},{2,4},{3,5},{4,6},{5,7},{6,0},{7,1},{8,10},{9,11},{10,... | collective-permute-start | bytes 245768 | tf_op jit(solution)/shard_map/ppermute | solution.py:30
  53.0 5.7 %collective-permute-start.16 = (f16[4,4,2560]{2,1,0:T(4,128)(2,1)S(1)}, f16[4,4,2560]{2,1,0:T(4,128)(2,1)S(1)}, u32[]{:S(2)}, u32[]{:S(2)}) collective-permute-start(f16[4,4,2560]{2,1,0:T(4,128)(2,1)S(1)} %get-tuple-element.107), channel_id=1, source_target_pairs={{0,6},{1,7},{2,0},{3,1},{4,2},{5,3},{6,4},{7,5},{8,14},{9,15},{10,... | collective-permute-start | bytes 245768 | tf_op jit(solution)/shard_map/ppermute | solution.py:30
  59.0 10.7 %copy-start = (f32[32,8192]{1,0:T(8,128)S(1)}, f32[32,8192]{1,0:T(8,128)}, u32[]{:S(2)}) copy-start(f32[32,8192]{1,0:T(8,128)} %frag_g.1) | copy-start | bytes 3145732
  59.0 10.7 %copy-start.1 = (f32[32,8192]{1,0:T(8,128)S(1)}, f32[32,8192]{1,0:T(8,128)}, u32[]{:S(2)}) copy-start(f32[32,8192]{1,0:T(8,128)} %param.9) | copy-start | bytes 3145732
  59.1 12.2 %collective-permute-start.18 = (f16[4,8192]{1,0:T(4,128)(2,1)S(1)}, f16[4,8192]{1,0:T(4,128)(2,1)S(1)}, u32[]{:S(2)}, u32[]{:S(2)}) collective-permute-start(f16[4,8192]{1,0:T(4,128)(2,1)S(1)} %get-tuple-element.120), channel_id=1, source_target_pairs={{0,16},{1,17},{2,18},{3,19},{4,20},{5,21},{6,22},{7,23},{8,24},{9,... | collective-permute-start | bytes 196616 | tf_op jit(solution)/shard_map/ppermute | solution.py:38
  62.4 8.9 %collective-permute-start.19 = (f16[4,8192]{1,0:T(4,128)(2,1)S(1)}, f16[4,8192]{1,0:T(4,128)(2,1)S(1)}, u32[]{:S(2)}, u32[]{:S(2)}) collective-permute-start(f16[4,8192]{1,0:T(4,128)(2,1)S(1)} %get-tuple-element.121), channel_id=1, source_target_pairs={{0,32},{1,33},{2,34},{3,35},{4,36},{5,37},{6,38},{7,39},{8,40},{9,... | collective-permute-start | bytes 196616 | tf_op jit(solution)/shard_map/ppermute | solution.py:38
  66.9 6.1 %collective-permute-start.20 = (f16[4,8192]{1,0:T(4,128)(2,1)S(1)}, f16[4,8192]{1,0:T(4,128)(2,1)S(1)}, u32[]{:S(2)}, u32[]{:S(2)}) collective-permute-start(f16[4,8192]{1,0:T(4,128)(2,1)S(1)} %get-tuple-element.122), channel_id=1, source_target_pairs={{0,48},{1,49},{2,50},{3,51},{4,52},{5,53},{6,54},{7,55},{8,56},{9,... | collective-permute-start | bytes 196616 | tf_op jit(solution)/shard_map/ppermute | solution.py:38
  69.7 3.3 %copy-start.2 = (f32[1,4,8192]{2,1,0:T(4,128)S(1)}, f32[1,4,8192]{2,1,0:T(4,128)}, u32[]{:S(2)}) copy-start(f32[1,4,8192]{2,1,0:T(4,128)} %param.11) | copy-start | bytes 393220
  69.7 3.3 %copy-start.3 = (f32[1,4,8192]{2,1,0:T(4,128)S(1)}, f32[1,4,8192]{2,1,0:T(4,128)}, u32[]{:S(2)}) copy-start(f32[1,4,8192]{2,1,0:T(4,128)} %param.12) | copy-start | bytes 393220
  69.7 3.3 %copy-start.4 = (f32[1,4,8192]{2,1,0:T(4,128)S(1)}, f32[1,4,8192]{2,1,0:T(4,128)}, u32[]{:S(2)}) copy-start(f32[1,4,8192]{2,1,0:T(4,128)} %param.13) | copy-start | bytes 393220

commit v3 on v2

--- a/solution.py
+++ b/solution.py
@@ -156,6 +156,32 @@
     )(*(pltpu.with_memory_space_constraint(x, pltpu.HBM) for x in (g, frag_g, frag_l)))
 
 
+def merge_kernel(a0, a1, a2, a3, b_own, b_part, c_own, c_part, a, b, c):
+    for i in range(NZ // 2):
+        for q in range(2):
+            total = a0[i, q].astype(F32)
+            for part in (a1, a2, a3):
+                total = total + part[i, q].astype(F32)
+            a[i, q] = total * 16.0
+            for j in range(NY):
+                c[i, q, j] = (c_own[i, q, j].astype(F32) + c_part[i, q, j].astype(F32)) * 32.0
+        for j in range(NY):
+            b[i, j] = (b_own[i, j].astype(F32) + b_part[i, j].astype(F32)) * 32.0
+
+
+def merge(*parts):
+    in_vmem = pl.BlockSpec(memory_space=pltpu.VMEM)
+    shapes = [parts[i].shape for i in (0, 4, 6)]
+    return pl.pallas_call(
+        merge_kernel,
+        out_shape=tuple(jax.ShapeDtypeStruct(shape, F32) for shape in shapes),
+        in_specs=[in_vmem] * 8,
+        out_specs=(in_vmem,) * 3,
+        compiler_params=pltpu.CompilerParams(vmem_limit_bytes=20 << 20),
+        cost_estimate=pl.CostEstimate(flops=2 << 20, bytes_accessed=8 << 20, transcendentals=0),
+    )(*parts)
+
+
 def sums(g, frag, f):
     z, y, h = f // (NY * NH), (f // NH) % NY, f % NH
     p, j = z % 2, z // 2
@@ -171,12 +197,7 @@
     a0, c_own, b_own, a_parts, c_part, b_part = together(
         (a0, c_own, b_own, a_parts, c_part, b_part)
     )
-    a = a0.astype(F32)
-    for part in a_parts:
-        a = a + part.astype(F32)
-    a = a * 16.0
-    b = (b_own.astype(F32) + b_part.astype(F32)) * 32.0
-    c = (c_own.astype(F32) + c_part.astype(F32)) * 32.0
+    a, b, c = merge(a0, *a_parts, b_own, b_part, c_own, c_part)
     a, a_send = rows_of(a, h, 2), rows_of(a, 1 - h, 2).astype(F16)
     b, b_sends = spread(b, y, NY, 1)
     c, c_send = take(c, p, 1), take(c, 1 - p, 1).astype(F16)

time: 74.2 us -> 73.7 us (level)
  other arithmetic: 8.45 us -> 5.32 us
  Pallas kernels: 3.79 us -> 5.72 us
  local copies, waits for them, and re-layouts: 0.03 us -> 0.86 us
    mul x3 -> x0, other arithmetic: 3.17 us -> none  [the longest x1 1.53 us: sums(): c = (c_own.astype(F32) + c_part.astype(F32)) * 32.0]
    pallas_call x0 -> x1, Pallas kernels: none -> 1.66 us  [merge(): pl.pallas_call(merge_kernel, out_shape=tuple((jax.ShapeDtypeStruct(shape,...]
    unnamed x10 -> x12, local copies, waits for them, and re-layouts: 0.03 us -> 0.86 us
  transfers between devices with their start and end apart: 21 -> 21, of which waited for: 13 -> 13; matrix products, arithmetic and copies ran while one was open for 9% -> 4% of each run, Pallas kernels for 0% -> 2%
where the time goes in v3:
time: 73.7 us; the launch traced here: 73.5 us
  starting transfers between devices  33.3 us (45%)
  waiting for transfers between devices  27.5 us (37%)
  Pallas kernels  5.72 us (8%)
  other arithmetic  5.32 us (7%)
  local copies, waits for them, and re-layouts  0.86 us (1%)
  between operations  0.84 us (1%)
    ppermute x9, waiting for transfers between devices, along_y(): return lax.ppermute(x, 'fsdp', perm_of(lambda z, y, h: (z, y + k, h)))  22.1 us
    ppermute x3, starting transfers between devices, along_z(): return lax.ppermute(x, 'fsdp', perm_of(lambda z, y, h: (z + k, y, h)))  10.5 us
    ppermute x9, starting transfers between devices, along_y(): return lax.ppermute(x, 'fsdp', perm_of(lambda z, y, h: (z, y + k, h)))  10 us
    ppermute x3, starting transfers between devices, along_h(): return lax.ppermute(x, 'fsdp', perm_of(lambda z, y, h: (z, y, h + 1)))  6.49 us
    ppermute x3, starting transfers between devices, pair_z(): lax.ppermute(x, 'fsdp', perm_of(lambda z, y, h: (((z + shift) % NZ ^ 1) -...  4.65 us
    pallas_call x1, Pallas kernels, deal(): pl.pallas_call(deal_kernel, out_shape=(a, a, a, a, c, c, b, b, half, half...  4.06 us
    ppermute x3, waiting for transfers between devices, along_h(): return lax.ppermute(x, 'fsdp', perm_of(lambda z, y, h: (z, y, h + 1)))  3.37 us
    ppermute x3, waiting for transfers between devices, along_z(): return lax.ppermute(x, 'fsdp', perm_of(lambda z, y, h: (z + k, y, h)))  1.69 us
  transfers between devices with their start and end apart: 21, of which 13 were waited for; matrix products, arithmetic and copies ran while one was open for 4% of the time, Pallas kernels for 2%

profile of v3, /device:TPU:24, one launch (start us, length us, event | category | flops | bytes accessed | tf_op | source)
XLA Modules:
  0.0 73.5 jit_solution(11035905797518516019)
XLA Ops:
  0.6 4.1 %shard_map.110 = (bf16[4,2,8,3072]{3,2,1,0:T(8,128)(2,1)}, bf16[4,2,8,3072]{3,2,1,0:T(8,128)(2,1)}, bf16[4,2,8,3072]{3,2,1,0:T(8,128)(2,1)}, bf16[4,2,8,3072]{3,...) custom-call(bf16[4,2,4,8,8192]{4,3,2,1,0:T(8,128)(2,1)} %bitcast.48,, ...), custom_call_target="tpu_custom_call" | custom-call | flops 2097152 | bytes 12582912 | tf_op jit(solution)/shard_map/pallas_call | solution.py:135
  4.7 0.8 %copy-done = bf16[4,4,8,2560]{3,2,1,0:T(8,128)(2,1)} copy-done((bf16[4,4,8,2560]{3,2,1,0:T(8,128)(2,1)}, bf16[4,4,8,2560]{3,2,1,0:T(8,128)(2,1)S(1)}, u32[]{:S(2)}) %copy-start) | copy-done | bytes 655384
  5.5 1.2 %collective-permute-start = (bf16[4,2,8,3072]{3,2,1,0:T(8,128)(2,1)}, bf16[4,2,8,3072]{3,2,1,0:T(8,128)(2,1)S(1)}, u32[]{:S(2)}, u32[]{:S(2)}) collective-permute-start(bf16[4,2,8,3072]{3,2,1,0:T(8,128)(2,1)} %get-tuple-element.70), channel_id=1, source_target_pairs={{0,4},{1,5},{2,6},{3,7},{4,0},{5,1},{6,2},{7,3},{8,12},{9,13},{10,... | collective-permute-start | bytes 1179656 | tf_op jit(solution)/shard_map/ppermute | solution.py:30
  6.8 2.2 %collective-permute-start.1 = (bf16[4,2,8,3072]{3,2,1,0:T(8,128)(2,1)}, bf16[4,2,8,3072]{3,2,1,0:T(8,128)(2,1)}, u32[]{:S(2)}, u32[]{:S(2)}) collective-permute-start(bf16[4,2,8,3072]{3,2,1,0:T(8,128)(2,1)} %get-tuple-element.71), channel_id=1, source_target_pairs={{0,2},{1,3},{2,4},{3,5},{4,6},{5,7},{6,0},{7,1},{8,10},{9,11},{10,... | collective-permute-start | bytes 1179656 | tf_op jit(solution)/shard_map/ppermute | solution.py:30
  9.0 3.0 %collective-permute-start.3 = (bf16[4,2,4,4,2560]{4,3,2,1,0:T(4,128)(2,1)}, bf16[4,2,4,4,2560]{4,3,2,1,0:T(4,128)(2,1)S(1)}, u32[]{:S(2)}, u32[]{:S(2)}) collective-permute-start(bf16[4,2,4,4,2560]{4,3,2,1,0:T(4,128)(2,1)} %get-tuple-element.73), channel_id=1, source_target_pairs={{0,1},{1,0},{2,3},{3,2},{4,5},{5,4},{6,7},{7,6},{8,9},{9,8},{10,11... | collective-permute-start | bytes 1966088 | tf_op jit(solution)/shard_map/ppermute | solution.py:34
  12.0 1.9 %collective-permute-start.4 = (bf16[4,4,8,2560]{3,2,1,0:T(8,128)(2,1)}, bf16[4,4,8,2560]{3,2,1,0:T(8,128)(2,1)S(1)}, u32[]{:S(2)}, u32[]{:S(2)}) collective-permute-start(bf16[4,4,8,2560]{3,2,1,0:T(8,128)(2,1)} %copy-done), channel_id=1, source_target_pairs={{0,8},{1,9},{2,10},{3,11},{4,12},{5,13},{6,14},{7,15},{8,0},{9,1},... | collective-permute-start | bytes 1966088 | tf_op jit(solution)/shard_map/ppermute | solution.py:42
  13.9 1.1 %multiply_convert_fusion = f16[16,8192]{1,0:T(8,128)(2,1)S(1)} fusion(f32[16,8192]{1,0:T(8,128)S(1)} %get-tuple-element.94, f32[16,8192]{1,0:T(8,128)} %collective-permute-done.10), kind=kLoop, calls=%fused_computation.8 | loop fusion | flops 393216 | bytes 1310720 | tf_op jit(solution)/shard_map/convert_element_type | solution.py:196
  15.0 4.2 %collective-permute-done.a1 = bf16[4,2,8,3072]{3,2,1,0:T(8,128)(2,1)S(1)} collective-permute-done((bf16[4,2,8,3072]{3,2,1,0:T(8,128)(2,1)}, bf16[4,2,8,3072]{3,2,1,0:T(8,128)(2,1)S(1)}, u32[]{:S(2)}, u32[]{:S(2)}) %collective-permute-start) | collective-permute-done | bytes 393248 | tf_op jit(solution)/shard_map/ppermute | solution.py:30
  19.2 1.5 %collective-permute-start.11 = (f16[16,8192]{1,0:T(8,128)(2,1)S(1)}, f16[16,8192]{1,0:T(8,128)(2,1)S(1)}, u32[]{:S(2)}, u32[]{:S(2)}) collective-permute-start(f16[16,8192]{1,0:T(8,128)(2,1)S(1)} %multiply_convert_fusion), channel_id=1, source_target_pairs={{0,128},{128,0},{64,192},{192,64},{1,129},{129,1},{65,193},{193,65... | collective-permute-start | bytes 786440 | tf_op jit(solution)/shard_map/ppermute | solution.py:207
  20.7 5.9 %collective-permute-done.1.a2 = bf16[4,2,8,3072]{3,2,1,0:T(8,128)(2,1)} collective-permute-done((bf16[4,2,8,3072]{3,2,1,0:T(8,128)(2,1)}, bf16[4,2,8,3072]{3,2,1,0:T(8,128)(2,1)}, u32[]{:S(2)}, u32[]{:S(2)}) %collective-permute-start.1) | collective-permute-done | bytes 393248 | tf_op jit(solution)/shard_map/ppermute | solution.py:30
  26.6 0.7 collective-permute-done.2.a3
  27.3 1.0 %collective-permute-done.3.c_part = bf16[4,2,4,4,2560]{4,3,2,1,0:T(4,128)(2,1)S(1)} collective-permute-done((bf16[4,2,4,4,2560]{4,3,2,1,0:T(4,128)(2,1)}, bf16[4,2,4,4,2560]{4,3,2,1,0:T(4,128)(2,1)S(1)}, u32[]{:S(2)}, u32[]{:S(2)}) %collective-permute-start.3) | collective-permute-done | bytes 655392 | tf_op jit(solution)/shard_map/ppermute | solution.py:34
  28.3 0.4 collective-permute-done.4.b_part
  28.7 1.7 %shard_map.111 = (f32[4,2,8,3072]{3,2,1,0:T(8,128)S(1)}, f32[4,4,8,2560]{3,2,1,0:T(8,128)S(1)}, f32[4,2,4,4,2560]{4,3,2,1,0:T(4,128)S(1)}) custom-call(bf16[4,2,8,3072]{3,2,1,0:T(8,128)(2,1)S(1)} %get-tuple-element.75.a0, bf16[4,2,8,3072]{3,2,1,0:T(8,128)(2,1)S(1)} %collective-permute-done.a1, bf16[4,2,8,3072]{3,2,1,0:T(8,128)(2,1)} %collective-permute-done.1.a2, ...), custom_call_target="tpu_custom_call" | custom-call | flops 2097152 | bytes 8388608 | tf_op jit(solution)/shard_map/pallas_call | solution.py:175
  30.3 0.2 select_convert_fusion
  30.6 0.2 fusion
  30.8 1.8 %collective-permute-start.9 = (f16[4,4,4,2560]{3,2,1,0:T(4,128)(2,1)S(1)}, f16[4,4,4,2560]{3,2,1,0:T(4,128)(2,1)S(1)}, u32[]{:S(2)}, u32[]{:S(2)}) collective-permute-start(f16[4,4,4,2560]{3,2,1,0:T(4,128)(2,1)S(1)} %get-tuple-element.93), channel_id=1, source_target_pairs={{0,8},{1,9},{2,10},{3,11},{4,12},{5,13},{6,14},{7,15},{8,0},{9,1},... | collective-permute-start | bytes 983048 | tf_op jit(solution)/shard_map/ppermute | solution.py:42
  32.6 2.8 %collective-permute-start.5 = (f16[4,2,4,3072]{3,2,1,0:T(4,128)(2,1)S(1)}, f16[4,2,4,3072]{3,2,1,0:T(4,128)(2,1)S(1)}, u32[]{:S(2)}, u32[]{:S(2)}) collective-permute-start(f16[4,2,4,3072]{3,2,1,0:T(4,128)(2,1)S(1)} %get-tuple-element.87), channel_id=1, source_target_pairs={{0,1},{1,0},{2,3},{3,2},{4,5},{5,4},{6,7},{7,6},{8,9},{9,8},{10,11... | collective-permute-start | bytes 589832 | tf_op jit(solution)/shard_map/ppermute | solution.py:34
  35.4 2.2 %collective-permute-start.6 = (f16[4,8,2560]{2,1,0:T(8,128)(2,1)S(1)}, f16[4,8,2560]{2,1,0:T(8,128)(2,1)S(1)}, u32[]{:S(2)}, u32[]{:S(2)}) collective-permute-start(f16[4,8,2560]{2,1,0:T(8,128)(2,1)S(1)} %get-tuple-element.89), channel_id=1, source_target_pairs={{0,4},{1,5},{2,6},{3,7},{4,0},{5,1},{6,2},{7,3},{8,12},{9,13},{10,... | collective-permute-start | bytes 491528 | tf_op jit(solution)/shard_map/ppermute | solution.py:30
  37.6 1.1 %collective-permute-start.7 = (f16[4,8,2560]{2,1,0:T(8,128)(2,1)S(1)}, f16[4,8,2560]{2,1,0:T(8,128)(2,1)S(1)}, u32[]{:S(2)}, u32[]{:S(2)}) collective-permute-start(f16[4,8,2560]{2,1,0:T(8,128)(2,1)S(1)} %get-tuple-element.90), channel_id=1, source_target_pairs={{0,2},{1,3},{2,4},{3,5},{4,6},{5,7},{6,0},{7,1},{8,10},{9,11},{10,... | collective-permute-start | bytes 491528 | tf_op jit(solution)/shard_map/ppermute | solution.py:30
  38.7 0.9 %collective-permute-start.8 = (f16[4,8,2560]{2,1,0:T(8,128)(2,1)S(1)}, f16[4,8,2560]{2,1,0:T(8,128)(2,1)S(1)}, u32[]{:S(2)}, u32[]{:S(2)}) collective-permute-start(f16[4,8,2560]{2,1,0:T(8,128)(2,1)S(1)} %get-tuple-element.91), channel_id=1, source_target_pairs={{0,6},{1,7},{2,0},{3,1},{4,2},{5,3},{6,4},{7,5},{8,14},{9,15},{10,... | collective-permute-start | bytes 491528 | tf_op jit(solution)/shard_map/ppermute | solution.py:30
  39.6 3.7 %collective-permute-done.6 = f16[4,8,2560]{2,1,0:T(8,128)(2,1)S(1)} collective-permute-done((f16[4,8,2560]{2,1,0:T(8,128)(2,1)S(1)}, f16[4,8,2560]{2,1,0:T(8,128)(2,1)S(1)}, u32[]{:S(2)}, u32[]{:S(2)}) %collective-permute-start.6) | collective-permute-done | bytes 163872 | tf_op jit(solution)/shard_map/ppermute | solution.py:30
  43.3 1.4 %collective-permute-done.7 = f16[4,8,2560]{2,1,0:T(8,128)(2,1)S(1)} collective-permute-done((f16[4,8,2560]{2,1,0:T(8,128)(2,1)S(1)}, f16[4,8,2560]{2,1,0:T(8,128)(2,1)S(1)}, u32[]{:S(2)}, u32[]{:S(2)}) %collective-permute-start.7) | collective-permute-done | bytes 163872 | tf_op jit(solution)/shard_map/ppermute | solution.py:30
  44.6 0.6 collective-permute-done.8
  45.2 0.1 add_multiply_fusion.2
  45.4 0.1 add_multiply_fusion.3
  45.6 0.2 add_multiply_fusion
  45.8 0.1 fusion.5
  45.9 0.1 add_multiply_fusion.1
  46.0 0.1 collective-permute-start.17
  46.1 0.7 collective-permute-start.13
  46.8 0.9 %collective-permute-start.12 = (f16[4,4,3072]{2,1,0:T(4,128)(2,1)S(1)}, f16[4,4,3072]{2,1,0:T(4,128)(2,1)S(1)}, u32[]{:S(2)}, u32[]{:S(2)}) collective-permute-start(f16[4,4,3072]{2,1,0:T(4,128)(2,1)S(1)} %get-tuple-element.107), channel_id=1, source_target_pairs={{0,8},{1,9},{2,10},{3,11},{4,12},{5,13},{6,14},{7,15},{8,0},{9,1},... | collective-permute-start | bytes 294920 | tf_op jit(solution)/shard_map/ppermute | solution.py:42
  47.7 1.0 %collective-permute-start.14 = (f16[4,4,2560]{2,1,0:T(4,128)(2,1)S(1)}, f16[4,4,2560]{2,1,0:T(4,128)(2,1)S(1)}, u32[]{:S(2)}, u32[]{:S(2)}) collective-permute-start(f16[4,4,2560]{2,1,0:T(4,128)(2,1)S(1)} %get-tuple-element.111), channel_id=1, source_target_pairs={{0,4},{1,5},{2,6},{3,7},{4,0},{5,1},{6,2},{7,3},{8,12},{9,13},{10,... | collective-permute-start | bytes 245768 | tf_op jit(solution)/shard_map/ppermute | solution.py:30
  48.7 1.4 %collective-permute-start.15 = (f16[4,4,2560]{2,1,0:T(4,128)(2,1)S(1)}, f16[4,4,2560]{2,1,0:T(4,128)(2,1)S(1)}, u32[]{:S(2)}, u32[]{:S(2)}) collective-permute-start(f16[4,4,2560]{2,1,0:T(4,128)(2,1)S(1)} %get-tuple-element.112), channel_id=1, source_target_pairs={{0,2},{1,3},{2,4},{3,5},{4,6},{5,7},{6,0},{7,1},{8,10},{9,11},{10,... | collective-permute-start | bytes 245768 | tf_op jit(solution)/shard_map/ppermute | solution.py:30
  50.1 2.4 %collective-permute-done.13 = f16[4,4,2560]{2,1,0:T(4,128)(2,1)S(1)} collective-permute-done((f16[4,4,2560]{2,1,0:T(4,128)(2,1)S(1)}, f16[4,4,2560]{2,1,0:T(4,128)(2,1)S(1)}, u32[]{:S(2)}, u32[]{:S(2)}) %collective-permute-start.13) | collective-permute-done | bytes 81952 | tf_op jit(solution)/shard_map/ppermute | solution.py:34
  52.5 1.1 %collective-permute-done.14 = f16[4,4,2560]{2,1,0:T(4,128)(2,1)S(1)} collective-permute-done((f16[4,4,2560]{2,1,0:T(4,128)(2,1)S(1)}, f16[4,4,2560]{2,1,0:T(4,128)(2,1)S(1)}, u32[]{:S(2)}, u32[]{:S(2)}) %collective-permute-start.14) | collective-permute-done | bytes 81952 | tf_op jit(solution)/shard_map/ppermute | solution.py:30
  53.6 0.7 collective-permute-done.15
  54.3 3.8 %collective-permute-done.16 = f16[4,4,2560]{2,1,0:T(4,128)(2,1)S(1)} collective-permute-done((f16[4,4,2560]{2,1,0:T(4,128)(2,1)S(1)}, f16[4,4,2560]{2,1,0:T(4,128)(2,1)S(1)}, u32[]{:S(2)}, u32[]{:S(2)}) %collective-permute-start.16) | collective-permute-done | bytes 81952 | tf_op jit(solution)/shard_map/ppermute | solution.py:30
  58.2 0.1 add_multiply_fusion.5
  58.4 0.1 pad_maximum_fusion
  58.5 0.1 fusion.10
  58.6 3.3 %collective-permute-start.18 = (f16[4,8192]{1,0:T(4,128)(2,1)S(1)}, f16[4,8192]{1,0:T(4,128)(2,1)S(1)}, u32[]{:S(2)}, u32[]{:S(2)}) collective-permute-start(f16[4,8192]{1,0:T(4,128)(2,1)S(1)} %get-tuple-element.126), channel_id=1, source_target_pairs={{0,16},{1,17},{2,18},{3,19},{4,20},{5,21},{6,22},{7,23},{8,24},{9,... | collective-permute-start | bytes 196616 | tf_op jit(solution)/shard_map/ppermute | solution.py:38
  62.0 4.5 %collective-permute-start.19 = (f16[4,8192]{1,0:T(4,128)(2,1)S(1)}, f16[4,8192]{1,0:T(4,128)(2,1)S(1)}, u32[]{:S(2)}, u32[]{:S(2)}) collective-permute-start(f16[4,8192]{1,0:T(4,128)(2,1)S(1)} %get-tuple-element.127), channel_id=1, source_target_pairs={{0,32},{1,33},{2,34},{3,35},{4,36},{5,37},{6,38},{7,39},{8,40},{9,... | collective-permute-start | bytes 196616 | tf_op jit(solution)/shard_map/ppermute | solution.py:38
  66.5 2.7 %collective-permute-start.20 = (f16[4,8192]{1,0:T(4,128)(2,1)S(1)}, f16[4,8192]{1,0:T(4,128)(2,1)S(1)}, u32[]{:S(2)}, u32[]{:S(2)}) collective-permute-start(f16[4,8192]{1,0:T(4,128)(2,1)S(1)} %get-tuple-element.128), channel_id=1, source_target_pairs={{0,48},{1,49},{2,50},{3,51},{4,52},{5,53},{6,54},{7,55},{8,56},{9,... | collective-permute-start | bytes 196616 | tf_op jit(solution)/shard_map/ppermute | solution.py:38
  69.1 0.1 broadcast_select_fusion.1
  69.2 1.6 %multiply_subtract_fusion = (f32[32,8192]{1,0:T(8,128)}, f32[32,8192]{1,0:T(8,128)}) fusion(f32[32,8192]{1,0:T(8,128)S(1)} %copy-done.1, f32[16,8192]{1,0:T(8,128)S(1)} %get-tuple-element.141, f32[16,8192]{1,0:T(8,128)S(1)} %get-tuple-element.140, f32[32,8192]{1,0:T(8,128)S(1)} %copy-done.2), kind=kLoop, calls=%fused_computation.1 | loop fusion | flops 2097152 | bytes 5242880 | tf_op jit(solution)/shard_map/sub | solution.py:246
  70.8 1.7 %collective-permute-done.20 = f16[4,8192]{1,0:T(4,128)(2,1)S(1)} collective-permute-done((f16[4,8192]{1,0:T(4,128)(2,1)S(1)}, f16[4,8192]{1,0:T(4,128)(2,1)S(1)}, u32[]{:S(2)}, u32[]{:S(2)}) %collective-permute-start.20) | collective-permute-done | bytes 65568 | tf_op jit(solution)/shard_map/ppermute | solution.py:38
  72.5 1.0 %multiply_subtract_fusion.1 = (f32[1,4,8192]{2,1,0:T(4,128)}, f32[1,4,8192]{2,1,0:T(4,128)}, f32[1,4,8192]{2,1,0:T(4,128)}) fusion(f32[1,4,8192]{2,1,0:T(4,128)S(1)} %copy-done.3, f16[4,8192]{1,0:T(4,128)(2,1)S(1)} %collective-permute-done.20, f16[4,8192]{1,0:T(4,128)(2,1)S(1)} %collective-permute-done.19, f32[4,8192]{1,0:T(4,128)S(1)} %get-tuple-element.125, ...), kind=kLoop, calls=%fused_computation.36 | loop fusion | flops 720896 | bytes 1114112 | tf_op jit(solution)/shard_map/sub | solution.py:252
  (27 shorter events, 0.3 us)
Async XLA Ops:
  4.7 0.8 %copy-start = (bf16[4,4,8,2560]{3,2,1,0:T(8,128)(2,1)}, bf16[4,4,8,2560]{3,2,1,0:T(8,128)(2,1)S(1)}, u32[]{:S(2)}) copy-start(bf16[4,4,8,2560]{3,2,1,0:T(8,128)(2,1)S(1)} %get-tuple-element.74) | copy-start | bytes 1966084
  5.5 6.5 %collective-permute-start.10 = (f32[16,8192]{1,0:T(8,128)}, f32[16,8192]{1,0:T(8,128)}, u32[]{:S(2)}, u32[]{:S(2)}) collective-permute-start(f32[16,8192]{1,0:T(8,128)} %get-tuple-element.95), channel_id=1, source_target_pairs={{0,64},{64,0},{128,192},{192,128},{1,65},{65,1},{129,193},{193,129... | collective-permute-start | bytes 1572872 | tf_op jit(solution)/shard_map/ppermute | solution.py:48
  5.5 13.7 %collective-permute-start = (bf16[4,2,8,3072]{3,2,1,0:T(8,128)(2,1)}, bf16[4,2,8,3072]{3,2,1,0:T(8,128)(2,1)S(1)}, u32[]{:S(2)}, u32[]{:S(2)}) collective-permute-start(bf16[4,2,8,3072]{3,2,1,0:T(8,128)(2,1)} %get-tuple-element.70), channel_id=1, source_target_pairs={{0,4},{1,5},{2,6},{3,7},{4,0},{5,1},{6,2},{7,3},{8,12},{9,13},{10,... | collective-permute-start | bytes 1179656 | tf_op jit(solution)/shard_map/ppermute | solution.py:30
  6.8 19.9 %collective-permute-start.1 = (bf16[4,2,8,3072]{3,2,1,0:T(8,128)(2,1)}, bf16[4,2,8,3072]{3,2,1,0:T(8,128)(2,1)}, u32[]{:S(2)}, u32[]{:S(2)}) collective-permute-start(bf16[4,2,8,3072]{3,2,1,0:T(8,128)(2,1)} %get-tuple-element.71), channel_id=1, source_target_pairs={{0,2},{1,3},{2,4},{3,5},{4,6},{5,7},{6,0},{7,1},{8,10},{9,11},{10,... | collective-permute-start | bytes 1179656 | tf_op jit(solution)/shard_map/ppermute | solution.py:30
  9.0 18.4 %collective-permute-start.2 = (bf16[4,2,8,3072]{3,2,1,0:T(8,128)(2,1)}, bf16[4,2,8,3072]{3,2,1,0:T(8,128)(2,1)}, u32[]{:S(2)}, u32[]{:S(2)}) collective-permute-start(bf16[4,2,8,3072]{3,2,1,0:T(8,128)(2,1)} %get-tuple-element.72), channel_id=1, source_target_pairs={{0,6},{1,7},{2,0},{3,1},{4,2},{5,3},{6,4},{7,5},{8,14},{9,15},{10,... | collective-permute-start | bytes 1179656 | tf_op jit(solution)/shard_map/ppermute | solution.py:30
  9.0 19.3 %collective-permute-start.3 = (bf16[4,2,4,4,2560]{4,3,2,1,0:T(4,128)(2,1)}, bf16[4,2,4,4,2560]{4,3,2,1,0:T(4,128)(2,1)S(1)}, u32[]{:S(2)}, u32[]{:S(2)}) collective-permute-start(bf16[4,2,4,4,2560]{4,3,2,1,0:T(4,128)(2,1)} %get-tuple-element.73), channel_id=1, source_target_pairs={{0,1},{1,0},{2,3},{3,2},{4,5},{5,4},{6,7},{7,6},{8,9},{9,8},{10,11... | collective-permute-start | bytes 1966088 | tf_op jit(solution)/shard_map/ppermute | solution.py:34
  12.0 16.7 %collective-permute-start.4 = (bf16[4,4,8,2560]{3,2,1,0:T(8,128)(2,1)}, bf16[4,4,8,2560]{3,2,1,0:T(8,128)(2,1)S(1)}, u32[]{:S(2)}, u32[]{:S(2)}) collective-permute-start(bf16[4,4,8,2560]{3,2,1,0:T(8,128)(2,1)} %copy-done), channel_id=1, source_target_pairs={{0,8},{1,9},{2,10},{3,11},{4,12},{5,13},{6,14},{7,15},{8,0},{9,1},... | collective-permute-start | bytes 1966088 | tf_op jit(solution)/shard_map/ppermute | solution.py:42
  19.2 19.5 %collective-permute-start.11 = (f16[16,8192]{1,0:T(8,128)(2,1)S(1)}, f16[16,8192]{1,0:T(8,128)(2,1)S(1)}, u32[]{:S(2)}, u32[]{:S(2)}) collective-permute-start(f16[16,8192]{1,0:T(8,128)(2,1)S(1)} %multiply_convert_fusion), channel_id=1, source_target_pairs={{0,128},{128,0},{64,192},{192,64},{1,129},{129,1},{65,193},{193,65... | collective-permute-start | bytes 786440 | tf_op jit(solution)/shard_map/ppermute | solution.py:207
  30.8 14.4 %collective-permute-start.9 = (f16[4,4,4,2560]{3,2,1,0:T(4,128)(2,1)S(1)}, f16[4,4,4,2560]{3,2,1,0:T(4,128)(2,1)S(1)}, u32[]{:S(2)}, u32[]{:S(2)}) collective-permute-start(f16[4,4,4,2560]{3,2,1,0:T(4,128)(2,1)S(1)} %get-tuple-element.93), channel_id=1, source_target_pairs={{0,8},{1,9},{2,10},{3,11},{4,12},{5,13},{6,14},{7,15},{8,0},{9,1},... | collective-permute-start | bytes 983048 | tf_op jit(solution)/shard_map/ppermute | solution.py:42
  32.6 12.6 %collective-permute-start.5 = (f16[4,2,4,3072]{3,2,1,0:T(4,128)(2,1)S(1)}, f16[4,2,4,3072]{3,2,1,0:T(4,128)(2,1)S(1)}, u32[]{:S(2)}, u32[]{:S(2)}) collective-permute-start(f16[4,2,4,3072]{3,2,1,0:T(4,128)(2,1)S(1)} %get-tuple-element.87), channel_id=1, source_target_pairs={{0,1},{1,0},{2,3},{3,2},{4,5},{5,4},{6,7},{7,6},{8,9},{9,8},{10,11... | collective-permute-start | bytes 589832 | tf_op jit(solution)/shard_map/ppermute | solution.py:34
  35.4 7.9 %collective-permute-start.6 = (f16[4,8,2560]{2,1,0:T(8,128)(2,1)S(1)}, f16[4,8,2560]{2,1,0:T(8,128)(2,1)S(1)}, u32[]{:S(2)}, u32[]{:S(2)}) collective-permute-start(f16[4,8,2560]{2,1,0:T(8,128)(2,1)S(1)} %get-tuple-element.89), channel_id=1, source_target_pairs={{0,4},{1,5},{2,6},{3,7},{4,0},{5,1},{6,2},{7,3},{8,12},{9,13},{10,... | collective-permute-start | bytes 491528 | tf_op jit(solution)/shard_map/ppermute | solution.py:30
  37.6 7.0 %collective-permute-start.7 = (f16[4,8,2560]{2,1,0:T(8,128)(2,1)S(1)}, f16[4,8,2560]{2,1,0:T(8,128)(2,1)S(1)}, u32[]{:S(2)}, u32[]{:S(2)}) collective-permute-start(f16[4,8,2560]{2,1,0:T(8,128)(2,1)S(1)} %get-tuple-element.90), channel_id=1, source_target_pairs={{0,2},{1,3},{2,4},{3,5},{4,6},{5,7},{6,0},{7,1},{8,10},{9,11},{10,... | collective-permute-start | bytes 491528 | tf_op jit(solution)/shard_map/ppermute | solution.py:30
  38.7 6.5 %collective-permute-start.8 = (f16[4,8,2560]{2,1,0:T(8,128)(2,1)S(1)}, f16[4,8,2560]{2,1,0:T(8,128)(2,1)S(1)}, u32[]{:S(2)}, u32[]{:S(2)}) collective-permute-start(f16[4,8,2560]{2,1,0:T(8,128)(2,1)S(1)} %get-tuple-element.91), channel_id=1, source_target_pairs={{0,6},{1,7},{2,0},{3,1},{4,2},{5,3},{6,4},{7,5},{8,14},{9,15},{10,... | collective-permute-start | bytes 491528 | tf_op jit(solution)/shard_map/ppermute | solution.py:30
  46.0 12.1 %collective-permute-start.17 = (f32[16,8192]{1,0:T(8,128)S(1)}, f32[16,8192]{1,0:T(8,128)S(1)}, u32[]{:S(2)}, u32[]{:S(2)}) collective-permute-start(f32[16,8192]{1,0:T(8,128)S(1)} %add_multiply_fusion.1), channel_id=1, source_target_pairs={{0,64},{64,0},{128,192},{192,128},{1,65},{65,1},{129,193},{193,129... | collective-permute-start | bytes 1572872 | tf_op jit(solution)/shard_map/ppermute | solution.py:48
  46.1 6.4 %collective-permute-start.13 = (f16[4,4,2560]{2,1,0:T(4,128)(2,1)S(1)}, f16[4,4,2560]{2,1,0:T(4,128)(2,1)S(1)}, u32[]{:S(2)}, u32[]{:S(2)}) collective-permute-start(f16[4,4,2560]{2,1,0:T(4,128)(2,1)S(1)} %get-tuple-element.109), channel_id=1, source_target_pairs={{0,1},{1,0},{2,3},{3,2},{4,5},{5,4},{6,7},{7,6},{8,9},{9,8},{10,11... | collective-permute-start | bytes 245768 | tf_op jit(solution)/shard_map/ppermute | solution.py:34
  46.8 11.4 %collective-permute-start.12 = (f16[4,4,3072]{2,1,0:T(4,128)(2,1)S(1)}, f16[4,4,3072]{2,1,0:T(4,128)(2,1)S(1)}, u32[]{:S(2)}, u32[]{:S(2)}) collective-permute-start(f16[4,4,3072]{2,1,0:T(4,128)(2,1)S(1)} %get-tuple-element.107), channel_id=1, source_target_pairs={{0,8},{1,9},{2,10},{3,11},{4,12},{5,13},{6,14},{7,15},{8,0},{9,1},... | collective-permute-start | bytes 294920 | tf_op jit(solution)/shard_map/ppermute | solution.py:42
  47.7 5.9 %collective-permute-start.14 = (f16[4,4,2560]{2,1,0:T(4,128)(2,1)S(1)}, f16[4,4,2560]{2,1,0:T(4,128)(2,1)S(1)}, u32[]{:S(2)}, u32[]{:S(2)}) collective-permute-start(f16[4,4,2560]{2,1,0:T(4,128)(2,1)S(1)} %get-tuple-element.111), channel_id=1, source_target_pairs={{0,4},{1,5},{2,6},{3,7},{4,0},{5,1},{6,2},{7,3},{8,12},{9,13},{10,... | collective-permute-start | bytes 245768 | tf_op jit(solution)/shard_map/ppermute | solution.py:30
  48.7 5.6 %collective-permute-start.15 = (f16[4,4,2560]{2,1,0:T(4,128)(2,1)S(1)}, f16[4,4,2560]{2,1,0:T(4,128)(2,1)S(1)}, u32[]{:S(2)}, u32[]{:S(2)}) collective-permute-start(f16[4,4,2560]{2,1,0:T(4,128)(2,1)S(1)} %get-tuple-element.112), channel_id=1, source_target_pairs={{0,2},{1,3},{2,4},{3,5},{4,6},{5,7},{6,0},{7,1},{8,10},{9,11},{10,... | collective-permute-start | bytes 245768 | tf_op jit(solution)/shard_map/ppermute | solution.py:30
  52.5 5.7 %collective-permute-start.16 = (f16[4,4,2560]{2,1,0:T(4,128)(2,1)S(1)}, f16[4,4,2560]{2,1,0:T(4,128)(2,1)S(1)}, u32[]{:S(2)}, u32[]{:S(2)}) collective-permute-start(f16[4,4,2560]{2,1,0:T(4,128)(2,1)S(1)} %get-tuple-element.113), channel_id=1, source_target_pairs={{0,6},{1,7},{2,0},{3,1},{4,2},{5,3},{6,4},{7,5},{8,14},{9,15},{10,... | collective-permute-start | bytes 245768 | tf_op jit(solution)/shard_map/ppermute | solution.py:30
  58.5 10.7 %copy-start.1 = (f32[32,8192]{1,0:T(8,128)S(1)}, f32[32,8192]{1,0:T(8,128)}, u32[]{:S(2)}) copy-start(f32[32,8192]{1,0:T(8,128)} %frag_g.1) | copy-start | bytes 3145732
  58.5 10.7 %copy-start.2 = (f32[32,8192]{1,0:T(8,128)S(1)}, f32[32,8192]{1,0:T(8,128)}, u32[]{:S(2)}) copy-start(f32[32,8192]{1,0:T(8,128)} %param.9) | copy-start | bytes 3145732
  58.6 12.2 %collective-permute-start.18 = (f16[4,8192]{1,0:T(4,128)(2,1)S(1)}, f16[4,8192]{1,0:T(4,128)(2,1)S(1)}, u32[]{:S(2)}, u32[]{:S(2)}) collective-permute-start(f16[4,8192]{1,0:T(4,128)(2,1)S(1)} %get-tuple-element.126), channel_id=1, source_target_pairs={{0,16},{1,17},{2,18},{3,19},{4,20},{5,21},{6,22},{7,23},{8,24},{9,... | collective-permute-start | bytes 196616 | tf_op jit(solution)/shard_map/ppermute | solution.py:38
  62.0 8.9 %collective-permute-start.19 = (f16[4,8192]{1,0:T(4,128)(2,1)S(1)}, f16[4,8192]{1,0:T(4,128)(2,1)S(1)}, u32[]{:S(2)}, u32[]{:S(2)}) collective-permute-start(f16[4,8192]{1,0:T(4,128)(2,1)S(1)} %get-tuple-element.127), channel_id=1, source_target_pairs={{0,32},{1,33},{2,34},{3,35},{4,36},{5,37},{6,38},{7,39},{8,40},{9,... | collective-permute-start | bytes 196616 | tf_op jit(solution)/shard_map/ppermute | solution.py:38
  66.5 6.1 %collective-permute-start.20 = (f16[4,8192]{1,0:T(4,128)(2,1)S(1)}, f16[4,8192]{1,0:T(4,128)(2,1)S(1)}, u32[]{:S(2)}, u32[]{:S(2)}) collective-permute-start(f16[4,8192]{1,0:T(4,128)(2,1)S(1)} %get-tuple-element.128), channel_id=1, source_target_pairs={{0,48},{1,49},{2,50},{3,51},{4,52},{5,53},{6,54},{7,55},{8,56},{9,... | collective-permute-start | bytes 196616 | tf_op jit(solution)/shard_map/ppermute | solution.py:38
  69.2 3.3 %copy-start.3 = (f32[1,4,8192]{2,1,0:T(4,128)S(1)}, f32[1,4,8192]{2,1,0:T(4,128)}, u32[]{:S(2)}) copy-start(f32[1,4,8192]{2,1,0:T(4,128)} %param.11) | copy-start | bytes 393220
  69.2 3.3 %copy-start.4 = (f32[1,4,8192]{2,1,0:T(4,128)S(1)}, f32[1,4,8192]{2,1,0:T(4,128)}, u32[]{:S(2)}) copy-start(f32[1,4,8192]{2,1,0:T(4,128)} %param.12) | copy-start | bytes 393220
  69.2 3.3 %copy-start.5 = (f32[1,4,8192]{2,1,0:T(4,128)S(1)}, f32[1,4,8192]{2,1,0:T(4,128)}, u32[]{:S(2)}) copy-start(f32[1,4,8192]{2,1,0:T(4,128)} %param.13) | copy-start | bytes 393220

commit v4 on v3

--- a/solution.py
+++ b/solution.py
@@ -231,7 +231,7 @@
     c = gather(c, c_parts, 0.25)
     t, t_sends = spread(jnp.concatenate([a, c, b], axis=-1), j, NZ // 2, 0)
     t, t_sends = together((t, t_sends))
-    t_parts = [along_z(x, 2 * (k + 1)) for k, x in enumerate(t_sends)]
+    t_parts = [along_z(t_sends[k - 1], 2 * k) for k in (1, 3, 2)]
     core = lax.rem(lax.axis_index("replica"), 2)
     low, high = jnp.where(core == 0, mine, theirs), jnp.where(core == 0, theirs, mine)
     return gather(t, t_parts, 0.25), jnp.concatenate([low, high], axis=0)

time: 73.7 us -> 74.1 us (level)
  no operation moved by 1% of the time
where the time goes in v4:
time: 74.1 us; the launch traced here: 73.4 us
  starting transfers between devices  33.3 us (45%)
  waiting for transfers between devices  27.4 us (37%)
  Pallas kernels  5.72 us (8%)
  other arithmetic  5.32 us (7%)
  local copies, waits for them, and re-layouts  0.86 us (1%)
  between operations  0.84 us (1%)
    ppermute x9, waiting for transfers between devices, along_y(): return lax.ppermute(x, 'fsdp', perm_of(lambda z, y, h: (z, y + k, h)))  22.1 us
    ppermute x3, starting transfers between devices, along_z(): return lax.ppermute(x, 'fsdp', perm_of(lambda z, y, h: (z + k, y, h)))  10.5 us
    ppermute x9, starting transfers between devices, along_y(): return lax.ppermute(x, 'fsdp', perm_of(lambda z, y, h: (z, y + k, h)))  10 us
    ppermute x3, starting transfers between devices, along_h(): return lax.ppermute(x, 'fsdp', perm_of(lambda z, y, h: (z, y, h + 1)))  6.49 us
    ppermute x3, starting transfers between devices, pair_z(): lax.ppermute(x, 'fsdp', perm_of(lambda z, y, h: (((z + shift) % NZ ^ 1) -...  4.65 us
    pallas_call x1, Pallas kernels, deal(): pl.pallas_call(deal_kernel, out_shape=(a, a, a, a, c, c, b, b, half, half...  4.06 us
    ppermute x3, waiting for transfers between devices, along_h(): return lax.ppermute(x, 'fsdp', perm_of(lambda z, y, h: (z, y, h + 1)))  3.37 us
    pallas_call x1, Pallas kernels, merge(): pl.pallas_call(merge_kernel, out_shape=tuple((jax.ShapeDtypeStruct(shape,...  1.66 us
  transfers between devices with their start and end apart: 21, of which 13 were waited for; matrix products, arithmetic and copies ran while one was open for 4% of the time, Pallas kernels for 2%

profile of v4, /device:TPU:24, one launch (start us, length us, event | category | flops | bytes accessed | tf_op | source)
XLA Modules:
  0.0 73.4 jit_solution(11780401849730138492)
XLA Ops:
  0.6 4.1 %shard_map.110 = (bf16[4,2,8,3072]{3,2,1,0:T(8,128)(2,1)}, bf16[4,2,8,3072]{3,2,1,0:T(8,128)(2,1)}, bf16[4,2,8,3072]{3,2,1,0:T(8,128)(2,1)}, bf16[4,2,8,3072]{3,...) custom-call(bf16[4,2,4,8,8192]{4,3,2,1,0:T(8,128)(2,1)} %bitcast.48,, ...), custom_call_target="tpu_custom_call" | custom-call | flops 2097152 | bytes 12582912 | tf_op jit(solution)/shard_map/pallas_call | solution.py:135
  4.7 0.8 %copy-done = bf16[4,4,8,2560]{3,2,1,0:T(8,128)(2,1)} copy-done((bf16[4,4,8,2560]{3,2,1,0:T(8,128)(2,1)}, bf16[4,4,8,2560]{3,2,1,0:T(8,128)(2,1)S(1)}, u32[]{:S(2)}) %copy-start) | copy-done | bytes 655384
  5.5 1.2 %collective-permute-start = (bf16[4,2,8,3072]{3,2,1,0:T(8,128)(2,1)}, bf16[4,2,8,3072]{3,2,1,0:T(8,128)(2,1)S(1)}, u32[]{:S(2)}, u32[]{:S(2)}) collective-permute-start(bf16[4,2,8,3072]{3,2,1,0:T(8,128)(2,1)} %get-tuple-element.70), channel_id=1, source_target_pairs={{0,4},{1,5},{2,6},{3,7},{4,0},{5,1},{6,2},{7,3},{8,12},{9,13},{10,... | collective-permute-start | bytes 1179656 | tf_op jit(solution)/shard_map/ppermute | solution.py:30
  6.8 2.2 %collective-permute-start.1 = (bf16[4,2,8,3072]{3,2,1,0:T(8,128)(2,1)}, bf16[4,2,8,3072]{3,2,1,0:T(8,128)(2,1)}, u32[]{:S(2)}, u32[]{:S(2)}) collective-permute-start(bf16[4,2,8,3072]{3,2,1,0:T(8,128)(2,1)} %get-tuple-element.71), channel_id=1, source_target_pairs={{0,2},{1,3},{2,4},{3,5},{4,6},{5,7},{6,0},{7,1},{8,10},{9,11},{10,... | collective-permute-start | bytes 1179656 | tf_op jit(solution)/shard_map/ppermute | solution.py:30
  9.0 3.0 %collective-permute-start.3 = (bf16[4,2,4,4,2560]{4,3,2,1,0:T(4,128)(2,1)}, bf16[4,2,4,4,2560]{4,3,2,1,0:T(4,128)(2,1)S(1)}, u32[]{:S(2)}, u32[]{:S(2)}) collective-permute-start(bf16[4,2,4,4,2560]{4,3,2,1,0:T(4,128)(2,1)} %get-tuple-element.73), channel_id=1, source_target_pairs={{0,1},{1,0},{2,3},{3,2},{4,5},{5,4},{6,7},{7,6},{8,9},{9,8},{10,11... | collective-permute-start | bytes 1966088 | tf_op jit(solution)/shard_map/ppermute | solution.py:34
  12.0 1.9 %collective-permute-start.4 = (bf16[4,4,8,2560]{3,2,1,0:T(8,128)(2,1)}, bf16[4,4,8,2560]{3,2,1,0:T(8,128)(2,1)S(1)}, u32[]{:S(2)}, u32[]{:S(2)}) collective-permute-start(bf16[4,4,8,2560]{3,2,1,0:T(8,128)(2,1)} %copy-done), channel_id=1, source_target_pairs={{0,8},{1,9},{2,10},{3,11},{4,12},{5,13},{6,14},{7,15},{8,0},{9,1},... | collective-permute-start | bytes 1966088 | tf_op jit(solution)/shard_map/ppermute | solution.py:42
  13.9 1.1 %multiply_convert_fusion = f16[16,8192]{1,0:T(8,128)(2,1)S(1)} fusion(f32[16,8192]{1,0:T(8,128)S(1)} %get-tuple-element.94, f32[16,8192]{1,0:T(8,128)} %collective-permute-done.10), kind=kLoop, calls=%fused_computation.8 | loop fusion | flops 393216 | bytes 1310720 | tf_op jit(solution)/shard_map/convert_element_type | solution.py:196
  15.0 4.2 %collective-permute-done.a1 = bf16[4,2,8,3072]{3,2,1,0:T(8,128)(2,1)S(1)} collective-permute-done((bf16[4,2,8,3072]{3,2,1,0:T(8,128)(2,1)}, bf16[4,2,8,3072]{3,2,1,0:T(8,128)(2,1)S(1)}, u32[]{:S(2)}, u32[]{:S(2)}) %collective-permute-start) | collective-permute-done | bytes 393248 | tf_op jit(solution)/shard_map/ppermute | solution.py:30
  19.2 1.5 %collective-permute-start.11 = (f16[16,8192]{1,0:T(8,128)(2,1)S(1)}, f16[16,8192]{1,0:T(8,128)(2,1)S(1)}, u32[]{:S(2)}, u32[]{:S(2)}) collective-permute-start(f16[16,8192]{1,0:T(8,128)(2,1)S(1)} %multiply_convert_fusion), channel_id=1, source_target_pairs={{0,128},{128,0},{64,192},{192,64},{1,129},{129,1},{65,193},{193,65... | collective-permute-start | bytes 786440 | tf_op jit(solution)/shard_map/ppermute | solution.py:207
  20.7 5.9 %collective-permute-done.1.a2 = bf16[4,2,8,3072]{3,2,1,0:T(8,128)(2,1)} collective-permute-done((bf16[4,2,8,3072]{3,2,1,0:T(8,128)(2,1)}, bf16[4,2,8,3072]{3,2,1,0:T(8,128)(2,1)}, u32[]{:S(2)}, u32[]{:S(2)}) %collective-permute-start.1) | collective-permute-done | bytes 393248 | tf_op jit(solution)/shard_map/ppermute | solution.py:30
  26.6 0.7 collective-permute-done.2.a3
  27.3 1.0 %collective-permute-done.3.c_part = bf16[4,2,4,4,2560]{4,3,2,1,0:T(4,128)(2,1)S(1)} collective-permute-done((bf16[4,2,4,4,2560]{4,3,2,1,0:T(4,128)(2,1)}, bf16[4,2,4,4,2560]{4,3,2,1,0:T(4,128)(2,1)S(1)}, u32[]{:S(2)}, u32[]{:S(2)}) %collective-permute-start.3) | collective-permute-done | bytes 655392 | tf_op jit(solution)/shard_map/ppermute | solution.py:34
  28.3 0.4 collective-permute-done.4.b_part
  28.7 1.7 %shard_map.111 = (f32[4,2,8,3072]{3,2,1,0:T(8,128)S(1)}, f32[4,4,8,2560]{3,2,1,0:T(8,128)S(1)}, f32[4,2,4,4,2560]{4,3,2,1,0:T(4,128)S(1)}) custom-call(bf16[4,2,8,3072]{3,2,1,0:T(8,128)(2,1)S(1)} %get-tuple-element.75.a0, bf16[4,2,8,3072]{3,2,1,0:T(8,128)(2,1)S(1)} %collective-permute-done.a1, bf16[4,2,8,3072]{3,2,1,0:T(8,128)(2,1)} %collective-permute-done.1.a2, ...), custom_call_target="tpu_custom_call" | custom-call | flops 2097152 | bytes 8388608 | tf_op jit(solution)/shard_map/pallas_call | solution.py:175
  30.3 0.2 select_convert_fusion
  30.6 0.2 fusion
  30.8 1.8 %collective-permute-start.9 = (f16[4,4,4,2560]{3,2,1,0:T(4,128)(2,1)S(1)}, f16[4,4,4,2560]{3,2,1,0:T(4,128)(2,1)S(1)}, u32[]{:S(2)}, u32[]{:S(2)}) collective-permute-start(f16[4,4,4,2560]{3,2,1,0:T(4,128)(2,1)S(1)} %get-tuple-element.93), channel_id=1, source_target_pairs={{0,8},{1,9},{2,10},{3,11},{4,12},{5,13},{6,14},{7,15},{8,0},{9,1},... | collective-permute-start | bytes 983048 | tf_op jit(solution)/shard_map/ppermute | solution.py:42
  32.6 2.8 %collective-permute-start.5 = (f16[4,2,4,3072]{3,2,1,0:T(4,128)(2,1)S(1)}, f16[4,2,4,3072]{3,2,1,0:T(4,128)(2,1)S(1)}, u32[]{:S(2)}, u32[]{:S(2)}) collective-permute-start(f16[4,2,4,3072]{3,2,1,0:T(4,128)(2,1)S(1)} %get-tuple-element.87), channel_id=1, source_target_pairs={{0,1},{1,0},{2,3},{3,2},{4,5},{5,4},{6,7},{7,6},{8,9},{9,8},{10,11... | collective-permute-start | bytes 589832 | tf_op jit(solution)/shard_map/ppermute | solution.py:34
  35.4 2.2 %collective-permute-start.6 = (f16[4,8,2560]{2,1,0:T(8,128)(2,1)S(1)}, f16[4,8,2560]{2,1,0:T(8,128)(2,1)S(1)}, u32[]{:S(2)}, u32[]{:S(2)}) collective-permute-start(f16[4,8,2560]{2,1,0:T(8,128)(2,1)S(1)} %get-tuple-element.89), channel_id=1, source_target_pairs={{0,4},{1,5},{2,6},{3,7},{4,0},{5,1},{6,2},{7,3},{8,12},{9,13},{10,... | collective-permute-start | bytes 491528 | tf_op jit(solution)/shard_map/ppermute | solution.py:30
  37.6 1.1 %collective-permute-start.7 = (f16[4,8,2560]{2,1,0:T(8,128)(2,1)S(1)}, f16[4,8,2560]{2,1,0:T(8,128)(2,1)S(1)}, u32[]{:S(2)}, u32[]{:S(2)}) collective-permute-start(f16[4,8,2560]{2,1,0:T(8,128)(2,1)S(1)} %get-tuple-element.90), channel_id=1, source_target_pairs={{0,2},{1,3},{2,4},{3,5},{4,6},{5,7},{6,0},{7,1},{8,10},{9,11},{10,... | collective-permute-start | bytes 491528 | tf_op jit(solution)/shard_map/ppermute | solution.py:30
  38.7 0.9 %collective-permute-start.8 = (f16[4,8,2560]{2,1,0:T(8,128)(2,1)S(1)}, f16[4,8,2560]{2,1,0:T(8,128)(2,1)S(1)}, u32[]{:S(2)}, u32[]{:S(2)}) collective-permute-start(f16[4,8,2560]{2,1,0:T(8,128)(2,1)S(1)} %get-tuple-element.91), channel_id=1, source_target_pairs={{0,6},{1,7},{2,0},{3,1},{4,2},{5,3},{6,4},{7,5},{8,14},{9,15},{10,... | collective-permute-start | bytes 491528 | tf_op jit(solution)/shard_map/ppermute | solution.py:30
  39.6 3.7 %collective-permute-done.6 = f16[4,8,2560]{2,1,0:T(8,128)(2,1)S(1)} collective-permute-done((f16[4,8,2560]{2,1,0:T(8,128)(2,1)S(1)}, f16[4,8,2560]{2,1,0:T(8,128)(2,1)S(1)}, u32[]{:S(2)}, u32[]{:S(2)}) %collective-permute-start.6) | collective-permute-done | bytes 163872 | tf_op jit(solution)/shard_map/ppermute | solution.py:30
  43.3 1.4 %collective-permute-done.7 = f16[4,8,2560]{2,1,0:T(8,128)(2,1)S(1)} collective-permute-done((f16[4,8,2560]{2,1,0:T(8,128)(2,1)S(1)}, f16[4,8,2560]{2,1,0:T(8,128)(2,1)S(1)}, u32[]{:S(2)}, u32[]{:S(2)}) %collective-permute-start.7) | collective-permute-done | bytes 163872 | tf_op jit(solution)/shard_map/ppermute | solution.py:30
  44.6 0.6 collective-permute-done.8
  45.2 0.1 add_multiply_fusion.2
  45.4 0.1 add_multiply_fusion.3
  45.6 0.2 add_multiply_fusion
  45.8 0.1 fusion.5
  45.9 0.1 add_multiply_fusion.1
  46.0 0.1 collective-permute-start.17
  46.1 0.7 collective-permute-start.13
  46.8 0.9 %collective-permute-start.12 = (f16[4,4,3072]{2,1,0:T(4,128)(2,1)S(1)}, f16[4,4,3072]{2,1,0:T(4,128)(2,1)S(1)}, u32[]{:S(2)}, u32[]{:S(2)}) collective-permute-start(f16[4,4,3072]{2,1,0:T(4,128)(2,1)S(1)} %get-tuple-element.107), channel_id=1, source_target_pairs={{0,8},{1,9},{2,10},{3,11},{4,12},{5,13},{6,14},{7,15},{8,0},{9,1},... | collective-permute-start | bytes 294920 | tf_op jit(solution)/shard_map/ppermute | solution.py:42
  47.7 1.0 %collective-permute-start.14 = (f16[4,4,2560]{2,1,0:T(4,128)(2,1)S(1)}, f16[4,4,2560]{2,1,0:T(4,128)(2,1)S(1)}, u32[]{:S(2)}, u32[]{:S(2)}) collective-permute-start(f16[4,4,2560]{2,1,0:T(4,128)(2,1)S(1)} %get-tuple-element.111), channel_id=1, source_target_pairs={{0,4},{1,5},{2,6},{3,7},{4,0},{5,1},{6,2},{7,3},{8,12},{9,13},{10,... | collective-permute-start | bytes 245768 | tf_op jit(solution)/shard_map/ppermute | solution.py:30
  48.7 1.4 %collective-permute-start.15 = (f16[4,4,2560]{2,1,0:T(4,128)(2,1)S(1)}, f16[4,4,2560]{2,1,0:T(4,128)(2,1)S(1)}, u32[]{:S(2)}, u32[]{:S(2)}) collective-permute-start(f16[4,4,2560]{2,1,0:T(4,128)(2,1)S(1)} %get-tuple-element.112), channel_id=1, source_target_pairs={{0,2},{1,3},{2,4},{3,5},{4,6},{5,7},{6,0},{7,1},{8,10},{9,11},{10,... | collective-permute-start | bytes 245768 | tf_op jit(solution)/shard_map/ppermute | solution.py:30
  50.1 2.4 %collective-permute-done.13 = f16[4,4,2560]{2,1,0:T(4,128)(2,1)S(1)} collective-permute-done((f16[4,4,2560]{2,1,0:T(4,128)(2,1)S(1)}, f16[4,4,2560]{2,1,0:T(4,128)(2,1)S(1)}, u32[]{:S(2)}, u32[]{:S(2)}) %collective-permute-start.13) | collective-permute-done | bytes 81952 | tf_op jit(solution)/shard_map/ppermute | solution.py:34
  52.5 1.1 %collective-permute-done.14 = f16[4,4,2560]{2,1,0:T(4,128)(2,1)S(1)} collective-permute-done((f16[4,4,2560]{2,1,0:T(4,128)(2,1)S(1)}, f16[4,4,2560]{2,1,0:T(4,128)(2,1)S(1)}, u32[]{:S(2)}, u32[]{:S(2)}) %collective-permute-start.14) | collective-permute-done | bytes 81952 | tf_op jit(solution)/shard_map/ppermute | solution.py:30
  53.6 0.7 collective-permute-done.15
  54.3 3.8 %collective-permute-done.16 = f16[4,4,2560]{2,1,0:T(4,128)(2,1)S(1)} collective-permute-done((f16[4,4,2560]{2,1,0:T(4,128)(2,1)S(1)}, f16[4,4,2560]{2,1,0:T(4,128)(2,1)S(1)}, u32[]{:S(2)}, u32[]{:S(2)}) %collective-permute-start.16) | collective-permute-done | bytes 81952 | tf_op jit(solution)/shard_map/ppermute | solution.py:30
  58.2 0.1 add_multiply_fusion.5
  58.4 0.1 pad_maximum_fusion
  58.5 0.1 fusion.10
  58.6 3.3 %collective-permute-start.18 = (f16[4,8192]{1,0:T(4,128)(2,1)S(1)}, f16[4,8192]{1,0:T(4,128)(2,1)S(1)}, u32[]{:S(2)}, u32[]{:S(2)}) collective-permute-start(f16[4,8192]{1,0:T(4,128)(2,1)S(1)} %get-tuple-element.126), channel_id=1, source_target_pairs={{0,16},{1,17},{2,18},{3,19},{4,20},{5,21},{6,22},{7,23},{8,24},{9,... | collective-permute-start | bytes 196616 | tf_op jit(solution)/shard_map/ppermute | solution.py:38
  62.0 2.2 %collective-permute-start.19 = (f16[4,8192]{1,0:T(4,128)(2,1)S(1)}, f16[4,8192]{1,0:T(4,128)(2,1)S(1)}, u32[]{:S(2)}, u32[]{:S(2)}) collective-permute-start(f16[4,8192]{1,0:T(4,128)(2,1)S(1)} %get-tuple-element.127), channel_id=1, source_target_pairs={{0,48},{1,49},{2,50},{3,51},{4,52},{5,53},{6,54},{7,55},{8,56},{9,... | collective-permute-start | bytes 196616 | tf_op jit(solution)/shard_map/ppermute | solution.py:38
  64.2 4.9 %collective-permute-start.20 = (f16[4,8192]{1,0:T(4,128)(2,1)S(1)}, f16[4,8192]{1,0:T(4,128)(2,1)S(1)}, u32[]{:S(2)}, u32[]{:S(2)}) collective-permute-start(f16[4,8192]{1,0:T(4,128)(2,1)S(1)} %get-tuple-element.128), channel_id=1, source_target_pairs={{0,32},{1,33},{2,34},{3,35},{4,36},{5,37},{6,38},{7,39},{8,40},{9,... | collective-permute-start | bytes 196616 | tf_op jit(solution)/shard_map/ppermute | solution.py:38
  69.1 0.1 broadcast_select_fusion.1
  69.2 1.6 %multiply_subtract_fusion = (f32[32,8192]{1,0:T(8,128)}, f32[32,8192]{1,0:T(8,128)}) fusion(f32[32,8192]{1,0:T(8,128)S(1)} %copy-done.1, f32[16,8192]{1,0:T(8,128)S(1)} %get-tuple-element.141, f32[16,8192]{1,0:T(8,128)S(1)} %get-tuple-element.140, f32[32,8192]{1,0:T(8,128)S(1)} %copy-done.2), kind=kLoop, calls=%fused_computation.1 | loop fusion | flops 2097152 | bytes 5242880 | tf_op jit(solution)/shard_map/sub | solution.py:246
  70.8 1.6 %collective-permute-done.20 = f16[4,8192]{1,0:T(4,128)(2,1)S(1)} collective-permute-done((f16[4,8192]{1,0:T(4,128)(2,1)S(1)}, f16[4,8192]{1,0:T(4,128)(2,1)S(1)}, u32[]{:S(2)}, u32[]{:S(2)}) %collective-permute-start.20) | collective-permute-done | bytes 65568 | tf_op jit(solution)/shard_map/ppermute | solution.py:38
  72.5 1.0 %multiply_subtract_fusion.1 = (f32[1,4,8192]{2,1,0:T(4,128)}, f32[1,4,8192]{2,1,0:T(4,128)}, f32[1,4,8192]{2,1,0:T(4,128)}) fusion(f32[1,4,8192]{2,1,0:T(4,128)S(1)} %copy-done.3, f16[4,8192]{1,0:T(4,128)(2,1)S(1)} %collective-permute-done.20, f16[4,8192]{1,0:T(4,128)(2,1)S(1)} %collective-permute-done.19, f32[4,8192]{1,0:T(4,128)S(1)} %get-tuple-element.125, ...), kind=kLoop, calls=%fused_computation.36 | loop fusion | flops 720896 | bytes 1114112 | tf_op jit(solution)/shard_map/sub | solution.py:252
  (27 shorter events, 0.3 us)
Async XLA Ops:
  4.7 0.8 %copy-start = (bf16[4,4,8,2560]{3,2,1,0:T(8,128)(2,1)}, bf16[4,4,8,2560]{3,2,1,0:T(8,128)(2,1)S(1)}, u32[]{:S(2)}) copy-start(bf16[4,4,8,2560]{3,2,1,0:T(8,128)(2,1)S(1)} %get-tuple-element.74) | copy-start | bytes 1966084
  5.5 6.5 %collective-permute-start.10 = (f32[16,8192]{1,0:T(8,128)}, f32[16,8192]{1,0:T(8,128)}, u32[]{:S(2)}, u32[]{:S(2)}) collective-permute-start(f32[16,8192]{1,0:T(8,128)} %get-tuple-element.95), channel_id=1, source_target_pairs={{0,64},{64,0},{128,192},{192,128},{1,65},{65,1},{129,193},{193,129... | collective-permute-start | bytes 1572872 | tf_op jit(solution)/shard_map/ppermute | solution.py:48
  5.5 13.7 %collective-permute-start = (bf16[4,2,8,3072]{3,2,1,0:T(8,128)(2,1)}, bf16[4,2,8,3072]{3,2,1,0:T(8,128)(2,1)S(1)}, u32[]{:S(2)}, u32[]{:S(2)}) collective-permute-start(bf16[4,2,8,3072]{3,2,1,0:T(8,128)(2,1)} %get-tuple-element.70), channel_id=1, source_target_pairs={{0,4},{1,5},{2,6},{3,7},{4,0},{5,1},{6,2},{7,3},{8,12},{9,13},{10,... | collective-permute-start | bytes 1179656 | tf_op jit(solution)/shard_map/ppermute | solution.py:30
  6.8 19.9 %collective-permute-start.1 = (bf16[4,2,8,3072]{3,2,1,0:T(8,128)(2,1)}, bf16[4,2,8,3072]{3,2,1,0:T(8,128)(2,1)}, u32[]{:S(2)}, u32[]{:S(2)}) collective-permute-start(bf16[4,2,8,3072]{3,2,1,0:T(8,128)(2,1)} %get-tuple-element.71), channel_id=1, source_target_pairs={{0,2},{1,3},{2,4},{3,5},{4,6},{5,7},{6,0},{7,1},{8,10},{9,11},{10,... | collective-permute-start | bytes 1179656 | tf_op jit(solution)/shard_map/ppermute | solution.py:30
  9.0 18.4 %collective-permute-start.2 = (bf16[4,2,8,3072]{3,2,1,0:T(8,128)(2,1)}, bf16[4,2,8,3072]{3,2,1,0:T(8,128)(2,1)}, u32[]{:S(2)}, u32[]{:S(2)}) collective-permute-start(bf16[4,2,8,3072]{3,2,1,0:T(8,128)(2,1)} %get-tuple-element.72), channel_id=1, source_target_pairs={{0,6},{1,7},{2,0},{3,1},{4,2},{5,3},{6,4},{7,5},{8,14},{9,15},{10,... | collective-permute-start | bytes 1179656 | tf_op jit(solution)/shard_map/ppermute | solution.py:30
  9.0 19.3 %collective-permute-start.3 = (bf16[4,2,4,4,2560]{4,3,2,1,0:T(4,128)(2,1)}, bf16[4,2,4,4,2560]{4,3,2,1,0:T(4,128)(2,1)S(1)}, u32[]{:S(2)}, u32[]{:S(2)}) collective-permute-start(bf16[4,2,4,4,2560]{4,3,2,1,0:T(4,128)(2,1)} %get-tuple-element.73), channel_id=1, source_target_pairs={{0,1},{1,0},{2,3},{3,2},{4,5},{5,4},{6,7},{7,6},{8,9},{9,8},{10,11... | collective-permute-start | bytes 1966088 | tf_op jit(solution)/shard_map/ppermute | solution.py:34
  12.0 16.7 %collective-permute-start.4 = (bf16[4,4,8,2560]{3,2,1,0:T(8,128)(2,1)}, bf16[4,4,8,2560]{3,2,1,0:T(8,128)(2,1)S(1)}, u32[]{:S(2)}, u32[]{:S(2)}) collective-permute-start(bf16[4,4,8,2560]{3,2,1,0:T(8,128)(2,1)} %copy-done), channel_id=1, source_target_pairs={{0,8},{1,9},{2,10},{3,11},{4,12},{5,13},{6,14},{7,15},{8,0},{9,1},... | collective-permute-start | bytes 1966088 | tf_op jit(solution)/shard_map/ppermute | solution.py:42
  19.2 19.5 %collective-permute-start.11 = (f16[16,8192]{1,0:T(8,128)(2,1)S(1)}, f16[16,8192]{1,0:T(8,128)(2,1)S(1)}, u32[]{:S(2)}, u32[]{:S(2)}) collective-permute-start(f16[16,8192]{1,0:T(8,128)(2,1)S(1)} %multiply_convert_fusion), channel_id=1, source_target_pairs={{0,128},{128,0},{64,192},{192,64},{1,129},{129,1},{65,193},{193,65... | collective-permute-start | bytes 786440 | tf_op jit(solution)/shard_map/ppermute | solution.py:207
  30.8 14.4 %collective-permute-start.9 = (f16[4,4,4,2560]{3,2,1,0:T(4,128)(2,1)S(1)}, f16[4,4,4,2560]{3,2,1,0:T(4,128)(2,1)S(1)}, u32[]{:S(2)}, u32[]{:S(2)}) collective-permute-start(f16[4,4,4,2560]{3,2,1,0:T(4,128)(2,1)S(1)} %get-tuple-element.93), channel_id=1, source_target_pairs={{0,8},{1,9},{2,10},{3,11},{4,12},{5,13},{6,14},{7,15},{8,0},{9,1},... | collective-permute-start | bytes 983048 | tf_op jit(solution)/shard_map/ppermute | solution.py:42
  32.6 12.6 %collective-permute-start.5 = (f16[4,2,4,3072]{3,2,1,0:T(4,128)(2,1)S(1)}, f16[4,2,4,3072]{3,2,1,0:T(4,128)(2,1)S(1)}, u32[]{:S(2)}, u32[]{:S(2)}) collective-permute-start(f16[4,2,4,3072]{3,2,1,0:T(4,128)(2,1)S(1)} %get-tuple-element.87), channel_id=1, source_target_pairs={{0,1},{1,0},{2,3},{3,2},{4,5},{5,4},{6,7},{7,6},{8,9},{9,8},{10,11... | collective-permute-start | bytes 589832 | tf_op jit(solution)/shard_map/ppermute | solution.py:34
  35.4 7.9 %collective-permute-start.6 = (f16[4,8,2560]{2,1,0:T(8,128)(2,1)S(1)}, f16[4,8,2560]{2,1,0:T(8,128)(2,1)S(1)}, u32[]{:S(2)}, u32[]{:S(2)}) collective-permute-start(f16[4,8,2560]{2,1,0:T(8,128)(2,1)S(1)} %get-tuple-element.89), channel_id=1, source_target_pairs={{0,4},{1,5},{2,6},{3,7},{4,0},{5,1},{6,2},{7,3},{8,12},{9,13},{10,... | collective-permute-start | bytes 491528 | tf_op jit(solution)/shard_map/ppermute | solution.py:30
  37.6 7.0 %collective-permute-start.7 = (f16[4,8,2560]{2,1,0:T(8,128)(2,1)S(1)}, f16[4,8,2560]{2,1,0:T(8,128)(2,1)S(1)}, u32[]{:S(2)}, u32[]{:S(2)}) collective-permute-start(f16[4,8,2560]{2,1,0:T(8,128)(2,1)S(1)} %get-tuple-element.90), channel_id=1, source_target_pairs={{0,2},{1,3},{2,4},{3,5},{4,6},{5,7},{6,0},{7,1},{8,10},{9,11},{10,... | collective-permute-start | bytes 491528 | tf_op jit(solution)/shard_map/ppermute | solution.py:30
  38.7 6.5 %collective-permute-start.8 = (f16[4,8,2560]{2,1,0:T(8,128)(2,1)S(1)}, f16[4,8,2560]{2,1,0:T(8,128)(2,1)S(1)}, u32[]{:S(2)}, u32[]{:S(2)}) collective-permute-start(f16[4,8,2560]{2,1,0:T(8,128)(2,1)S(1)} %get-tuple-element.91), channel_id=1, source_target_pairs={{0,6},{1,7},{2,0},{3,1},{4,2},{5,3},{6,4},{7,5},{8,14},{9,15},{10,... | collective-permute-start | bytes 491528 | tf_op jit(solution)/shard_map/ppermute | solution.py:30
  46.0 12.1 %collective-permute-start.17 = (f32[16,8192]{1,0:T(8,128)S(1)}, f32[16,8192]{1,0:T(8,128)S(1)}, u32[]{:S(2)}, u32[]{:S(2)}) collective-permute-start(f32[16,8192]{1,0:T(8,128)S(1)} %add_multiply_fusion.1), channel_id=1, source_target_pairs={{0,64},{64,0},{128,192},{192,128},{1,65},{65,1},{129,193},{193,129... | collective-permute-start | bytes 1572872 | tf_op jit(solution)/shard_map/ppermute | solution.py:48
  46.1 6.4 %collective-permute-start.13 = (f16[4,4,2560]{2,1,0:T(4,128)(2,1)S(1)}, f16[4,4,2560]{2,1,0:T(4,128)(2,1)S(1)}, u32[]{:S(2)}, u32[]{:S(2)}) collective-permute-start(f16[4,4,2560]{2,1,0:T(4,128)(2,1)S(1)} %get-tuple-element.109), channel_id=1, source_target_pairs={{0,1},{1,0},{2,3},{3,2},{4,5},{5,4},{6,7},{7,6},{8,9},{9,8},{10,11... | collective-permute-start | bytes 245768 | tf_op jit(solution)/shard_map/ppermute | solution.py:34
  46.8 11.4 %collective-permute-start.12 = (f16[4,4,3072]{2,1,0:T(4,128)(2,1)S(1)}, f16[4,4,3072]{2,1,0:T(4,128)(2,1)S(1)}, u32[]{:S(2)}, u32[]{:S(2)}) collective-permute-start(f16[4,4,3072]{2,1,0:T(4,128)(2,1)S(1)} %get-tuple-element.107), channel_id=1, source_target_pairs={{0,8},{1,9},{2,10},{3,11},{4,12},{5,13},{6,14},{7,15},{8,0},{9,1},... | collective-permute-start | bytes 294920 | tf_op jit(solution)/shard_map/ppermute | solution.py:42
  47.7 5.9 %collective-permute-start.14 = (f16[4,4,2560]{2,1,0:T(4,128)(2,1)S(1)}, f16[4,4,2560]{2,1,0:T(4,128)(2,1)S(1)}, u32[]{:S(2)}, u32[]{:S(2)}) collective-permute-start(f16[4,4,2560]{2,1,0:T(4,128)(2,1)S(1)} %get-tuple-element.111), channel_id=1, source_target_pairs={{0,4},{1,5},{2,6},{3,7},{4,0},{5,1},{6,2},{7,3},{8,12},{9,13},{10,... | collective-permute-start | bytes 245768 | tf_op jit(solution)/shard_map/ppermute | solution.py:30
  48.7 5.6 %collective-permute-start.15 = (f16[4,4,2560]{2,1,0:T(4,128)(2,1)S(1)}, f16[4,4,2560]{2,1,0:T(4,128)(2,1)S(1)}, u32[]{:S(2)}, u32[]{:S(2)}) collective-permute-start(f16[4,4,2560]{2,1,0:T(4,128)(2,1)S(1)} %get-tuple-element.112), channel_id=1, source_target_pairs={{0,2},{1,3},{2,4},{3,5},{4,6},{5,7},{6,0},{7,1},{8,10},{9,11},{10,... | collective-permute-start | bytes 245768 | tf_op jit(solution)/shard_map/ppermute | solution.py:30
  52.5 5.7 %collective-permute-start.16 = (f16[4,4,2560]{2,1,0:T(4,128)(2,1)S(1)}, f16[4,4,2560]{2,1,0:T(4,128)(2,1)S(1)}, u32[]{:S(2)}, u32[]{:S(2)}) collective-permute-start(f16[4,4,2560]{2,1,0:T(4,128)(2,1)S(1)} %get-tuple-element.113), channel_id=1, source_target_pairs={{0,6},{1,7},{2,0},{3,1},{4,2},{5,3},{6,4},{7,5},{8,14},{9,15},{10,... | collective-permute-start | bytes 245768 | tf_op jit(solution)/shard_map/ppermute | solution.py:30
  58.5 10.7 %copy-start.1 = (f32[32,8192]{1,0:T(8,128)S(1)}, f32[32,8192]{1,0:T(8,128)}, u32[]{:S(2)}) copy-start(f32[32,8192]{1,0:T(8,128)} %frag_g.1) | copy-start | bytes 3145732
  58.5 10.7 %copy-start.2 = (f32[32,8192]{1,0:T(8,128)S(1)}, f32[32,8192]{1,0:T(8,128)}, u32[]{:S(2)}) copy-start(f32[32,8192]{1,0:T(8,128)} %param.9) | copy-start | bytes 3145732
  58.6 12.2 %collective-permute-start.18 = (f16[4,8192]{1,0:T(4,128)(2,1)S(1)}, f16[4,8192]{1,0:T(4,128)(2,1)S(1)}, u32[]{:S(2)}, u32[]{:S(2)}) collective-permute-start(f16[4,8192]{1,0:T(4,128)(2,1)S(1)} %get-tuple-element.126), channel_id=1, source_target_pairs={{0,16},{1,17},{2,18},{3,19},{4,20},{5,21},{6,22},{7,23},{8,24},{9,... | collective-permute-start | bytes 196616 | tf_op jit(solution)/shard_map/ppermute | solution.py:38
  62.0 8.9 %collective-permute-start.19 = (f16[4,8192]{1,0:T(4,128)(2,1)S(1)}, f16[4,8192]{1,0:T(4,128)(2,1)S(1)}, u32[]{:S(2)}, u32[]{:S(2)}) collective-permute-start(f16[4,8192]{1,0:T(4,128)(2,1)S(1)} %get-tuple-element.127), channel_id=1, source_target_pairs={{0,48},{1,49},{2,50},{3,51},{4,52},{5,53},{6,54},{7,55},{8,56},{9,... | collective-permute-start | bytes 196616 | tf_op jit(solution)/shard_map/ppermute | solution.py:38
  64.2 8.3 %collective-permute-start.20 = (f16[4,8192]{1,0:T(4,128)(2,1)S(1)}, f16[4,8192]{1,0:T(4,128)(2,1)S(1)}, u32[]{:S(2)}, u32[]{:S(2)}) collective-permute-start(f16[4,8192]{1,0:T(4,128)(2,1)S(1)} %get-tuple-element.128), channel_id=1, source_target_pairs={{0,32},{1,33},{2,34},{3,35},{4,36},{5,37},{6,38},{7,39},{8,40},{9,... | collective-permute-start | bytes 196616 | tf_op jit(solution)/shard_map/ppermute | solution.py:38
  69.2 3.2 %copy-start.3 = (f32[1,4,8192]{2,1,0:T(4,128)S(1)}, f32[1,4,8192]{2,1,0:T(4,128)}, u32[]{:S(2)}) copy-start(f32[1,4,8192]{2,1,0:T(4,128)} %param.11) | copy-start | bytes 393220
  69.2 3.2 %copy-start.4 = (f32[1,4,8192]{2,1,0:T(4,128)S(1)}, f32[1,4,8192]{2,1,0:T(4,128)}, u32[]{:S(2)}) copy-start(f32[1,4,8192]{2,1,0:T(4,128)} %param.12) | copy-start | bytes 393220
  69.2 3.2 %copy-start.5 = (f32[1,4,8192]{2,1,0:T(4,128)S(1)}, f32[1,4,8192]{2,1,0:T(4,128)}, u32[]{:S(2)}) copy-start(f32[1,4,8192]{2,1,0:T(4,128)} %param.13) | copy-start | bytes 393220
